TPU v7x, 512 devices: a whole 4x4x16 slice. The times are simulated.
512 devices in a mesh: dp: 2 (over x_hi), seq: 32 (over z, core), tensor: 8 (over x_lo, y).
Axes of the slice: x: 4 (x_hi: 2, x_lo: 2; x = x_hi * 2 + x_lo), y: 4, z: 16, core: 2. Of those that a mesh axis runs over, the one named last changes fastest.
Arguments:
- queries: bfloat16 [32768, 64, 128], P(('dp', 'seq'), 'tensor'), parts along dimension 0, may hold values from -24 to 24
- keys: bfloat16 [32768, 64, 128], P(('dp', 'seq'), 'tensor'), parts along dimension 0, may hold values from -24 to 24
- values: bfloat16 [32768, 64, 128], P(('dp', 'seq'), 'tensor'), parts along dimension 0, may hold values from -6 to 6
- window_radius: int32 [128], P(('dp', 'tensor')), parts along dimension 0, may hold values from 1 to 3
- global_ids: int32 [4], P('dp'), parts along dimension 0, may hold values from 0 to 255, as said below
- rand_owner: int32 [8, 512, 8, 3], P('tensor', ('dp', 'seq')), parts along dimension 1, may hold values from 0 to 31, all different within a row; in each aligned block of 64 rows (0 to 63, 64 to 127, ..., all dimensions but the last counted through in order) at most 9 rows name the same one
- rand_local: int32 [8, 512, 8, 3], P('tensor', ('dp', 'seq')), parts along dimension 1, may hold values from 0 to 7
Outputs:
- attended: bfloat16 [32768, 64, 128], P(('dp', 'seq'), 'tensor'), parts along dimension 0
There are 2 independent parts, one for each index of `dp`. A program takes and returns all parts, laid end to end along the dimension named above; each array names one. Nothing has to cross between parts.
Inputs may be any that keep to these rules, and one draw needn't show every extreme that they name: `rand_owner`: for the query blocks of one index of seq and the heads of one group, at most 9 random blocks lie in one run; the 3 runs of one query block and head differ. `global_ids`: 2 different block numbers; the last block, 255, is always among them.
All inputs are finite; a program needn't handle non-finite values.
Results may differ from a plain program's by a relative error of at most 0.0046.
Values may be sent and summed in bfloat16 or wider, within the bound.
A program may use at most 128 MiB of HBM per device.

v0:
```python
import math

import jax
import jax.numpy as jnp
from jax import lax
from jax.sharding import PartitionSpec as P

BLOCK = 64
WIN = 3
G = 2
R = 3
NB_DEV = 8


def with_halo(block, sides, width):
    for axis, dim in sides:
        count = lax.axis_size(axis)
        forward = [(i, i + 1) for i in range(count - 1)]
        backward = [(target, source) for source, target in forward]
        low = lax.ppermute(
            lax.slice_in_dim(block, block.shape[dim] - width, None, axis=dim), axis, forward
        )
        high = lax.ppermute(lax.slice_in_dim(block, 0, width, axis=dim), axis, backward)
        block = jnp.concatenate([low, block, high], axis=dim)
    return block


def slot_rank(owners):
    length = owners.shape[-1]
    same_owner = owners[..., :, None] == owners[..., None, :]
    earlier = jnp.arange(length)[:, None] < jnp.arange(length)[None, :]
    return jnp.sum((same_owner & earlier).astype(jnp.int32), axis=-2)


def local(queries, keys, values, window_radius, global_ids, rand_owner, rand_local):
    local_blocks = NB_DEV
    block_rows = BLOCK
    local_rows, head_count, head_width = queries.shape
    shards = lax.axis_size("seq")
    position = lax.axis_index("seq")
    total_blocks = local_blocks * shards
    capacity = max(2, 3 * local_blocks * head_count * R // shards // 2)
    score_scale = 1.0 / math.sqrt(head_width)
    stacked = jnp.stack((keys, values), axis=0)
    padded = with_halo(stacked, (("seq", 1),), WIN * block_rows)
    padded = padded.reshape(
        2, local_blocks + 2 * WIN, block_rows, head_count, head_width
    ).transpose(3, 0, 1, 2, 4)
    blocks_query = queries.reshape(local_blocks, block_rows, head_count, head_width)
    blocks_pair = stacked.reshape(2, local_blocks, block_rows, head_count, head_width)
    block_ids = position * local_blocks + jnp.arange(local_blocks, dtype=jnp.int32)
    triples = jnp.concatenate((blocks_query[None], blocks_pair), axis=0)
    selector = (global_ids[:, None] == block_ids[None, :]).astype(jnp.bfloat16)
    flat_triples = triples.reshape(3, local_blocks, block_rows * head_count * head_width)
    picked = jnp.einsum("gb,tbf->tgf", selector, flat_triples, preferred_element_type=jnp.float32)
    summed = lax.psum(picked.astype(jnp.bfloat16), "seq")
    chosen = summed.reshape(3, G, block_rows, head_count, head_width)
    global_query, global_key, global_value = (chosen[0], chosen[1], chosen[2])
    global_scores = (
        jnp.einsum("gthd,shd->hgts", global_query, keys, preferred_element_type=jnp.float32)
        * score_scale
    )
    local_peak = jnp.max(global_scores, axis=-1)
    global_peak = lax.pmax(local_peak, "seq")
    global_weights = jnp.exp(global_scores - global_peak[..., None])
    local_total = jnp.sum(global_weights, axis=-1)
    local_weighted = jnp.einsum(
        "hgts,shd->hgtd",
        global_weights.astype(jnp.bfloat16),
        values,
        preferred_element_type=jnp.float32,
    )
    global_total, global_weighted = lax.psum((local_total, local_weighted), "seq")
    global_out = (global_weighted / global_total[..., None]).astype(jnp.bfloat16)
    owners = rand_owner[0].reshape(-1)
    places = rand_local[0].reshape(-1)
    head_index = jnp.broadcast_to(
        jnp.arange(head_count, dtype=jnp.int32)[None, :, None], (local_blocks, head_count, R)
    ).reshape(-1)
    slot_codes = head_index * local_blocks + places
    slot_ranks = slot_rank(owners)
    flat_pairs = blocks_pair.transpose(1, 3, 0, 2, 4)
    requested = jnp.zeros((shards, capacity), jnp.int32).at[owners, slot_ranks].set(slot_codes)
    wanted = lax.all_to_all(requested, "seq", split_axis=0, concat_axis=0, tiled=True)
    arrived = lax.all_to_all(
        flat_pairs[wanted % local_blocks, wanted // local_blocks],
        "seq",
        split_axis=0,
        concat_axis=0,
        tiled=True,
    )
    fetched = arrived[owners, slot_ranks].reshape(
        local_blocks, head_count, R, 2, block_rows, head_width
    )
    fetched = fetched.transpose(1, 3, 0, 2, 4, 5)
    offsets = jnp.arange(-WIN, WIN + 1, dtype=jnp.int32)
    window_blocks = block_ids[:, None] + offsets[None, :]
    inside = (window_blocks >= 0) & (window_blocks < total_blocks)
    global_pairs = jnp.stack((global_key, global_value), axis=0).transpose(3, 0, 1, 2, 4)
    query_heads = blocks_query.transpose(2, 0, 1, 3)

    def one_head(items):
        query_head, pad_head, global_head, random_head, radius = items
        windows = jnp.stack(
            [pad_head[:, offset : offset + local_blocks] for offset in range(2 * WIN + 1)], axis=2
        )
        global_keys = jnp.broadcast_to(
            global_head[:, None], (2, local_blocks, G, block_rows, head_width)
        )
        gathered = jnp.concatenate((windows, global_keys, random_head), axis=2)
        scores = (
            jnp.einsum(
                "btd,bkjd->btkj", query_head, gathered[0], preferred_element_type=jnp.float32
            )
            * score_scale
        )
        usable = jnp.concatenate(
            (
                inside & (jnp.abs(offsets) <= radius)[None, :],
                jnp.ones((local_blocks, G + R), jnp.bool_),
            ),
            axis=1,
        )
        usable_mask = usable[:, None, :, None]
        row_peak = jnp.max(jnp.where(usable_mask, scores, -jnp.inf), axis=(2, 3), keepdims=True)
        weights = jnp.where(usable_mask, jnp.exp(scores - row_peak), 0.0)
        row_total = jnp.sum(weights, axis=(2, 3))
        weighted = jnp.einsum(
            "btkj,bkjd->btd",
            weights.astype(jnp.bfloat16),
            gathered[1],
            preferred_element_type=jnp.float32,
        )
        return (weighted / row_total[..., None]).astype(jnp.bfloat16)

    sparse = lax.map(one_head, (query_heads, padded, global_pairs, fetched, window_radius))
    result = sparse.transpose(1, 2, 0, 3)
    for global_slot in range(G):
        owned = global_ids[global_slot] == block_ids
        result = jnp.where(
            owned[:, None, None, None], global_out[:, global_slot].transpose(1, 0, 2)[None], result
        )
    return result.reshape(local_rows, head_count, head_width)


def solution(mesh):
    placed = (
        P(("dp", "seq"), "tensor", None),
        P(("dp", "seq"), "tensor", None),
        P(("dp", "seq"), "tensor", None),
        P(("dp", "tensor")),
        P("dp"),
        P("tensor", ("dp", "seq"), None, None),
        P("tensor", ("dp", "seq"), None, None),
    )
    return jax.shard_map(
        local,
        mesh=mesh,
        in_specs=placed,
        out_specs=P(("dp", "seq"), "tensor", None),
        check_vma=False,
    )
```

profile of v0, /device:TPU:1, one launch (start us, length us, event | category | flops | bytes accessed | tf_op | source)
XLA Modules:
  0.0 848.1 jit_solution(13966316372036121370)
XLA Ops:
  9.1 10.5 %scatter_fusion = s32[32,9]{0,1:T(8,128)S(1)} fusion(s32[32,9]{0,1:T(8,128)S(1)} %broadcast.216, s32[192]{0:T(256)S(1)} %bitcast.211, s32[192]{0:T(256)S(1)} %add.134), kind=kCustom, calls=%fused_computation.2 | custom fusion | bytes 3840 | tf_op jit(solution)/shard_map/scatter | solution.py:83
  20.2 16.7 %all-to-all-start = ((s32[32,1,9]{2,1,0:T(1,128)}), s32[32,1,9]{2,1,0:T(1,128)S(1)}, u32[]{:S(2)}, u32[]{:S(2)}) async-start(s32[32,1,9]{2,1,0:T(1,128)} %copy.106), calls=%async_computation | async-start | bytes 32768 | tf_op jit(solution)/shard_map/all_to_all | solution.py:84
  37.8 10.9 %all-to-all-done = s32[32,1,9]{2,1,0:T(1,128)S(1)} async-done(((s32[32,1,9]{2,1,0:T(1,128)}), s32[32,1,9]{2,1,0:T(1,128)S(1)}, u32[]{:S(2)}, u32[]{:S(2)}) %all-to-all-start) | async-done | bytes 1184 | tf_op jit(solution)/shard_map/all_to_all | solution.py:84
  48.8 19.6 %gather_fusion = bf16[288,2,64,128]{3,2,1,0:T(8,128)(2,1)} fusion(bf16[8,8,2,64,128]{4,3,2,1,0:T(8,128)(2,1)S(1)} %maximum_bitcast_fusion, s32[288]{0:T(512)S(1)} %reshape.249), kind=kCustom, calls=%fused_computation | custom fusion | bytes 18876672 | tf_op jit(solution)/shard_map/gather | solution.py:86
  68.4 5.9 all-to-all-start.1
  74.4 1.4 stack.57
  75.9 1.4 stack.58
  77.3 1.4 concatenate.27
  78.7 3.8 fusion.43
  83.9 3.5 collective-permute-start
  87.5 1.9 collective-permute-start.1
  92.3 307.5 %all-reduce.4.cloned.1.call-done = bf16[3,2,65536]{2,1,0:T(2,128)(2,1)} async-done(((bf16[3,2,65536]{2,1,0:T(2,128)(2,1)}), bf16[3,2,65536]{2,1,0:T(2,128)(2,1)}) %all-reduce.4.cloned.1.call-update) | async-done | bytes 786448 | tf_op jit(solution)/shard_map/psum | solution.py:56
  399.7 1.6 slice_bitcast_fusion.23
  401.6 1.8 multiply_reduce_fusion
  403.4 135.4 %pmax.7 = f32[8,2,64]{2,1,0:T(2,128)S(1)} all-reduce(f32[8,2,64]{2,1,0:T(2,128)S(1)} %get-tuple-element.201), channel_id=1, replica_groups=mesh['dp'=2,'seq'=32,'tensor'=8] {'seq'}, use_global_device_ids=true, to_apply=%region_2.0 | all-reduce | flops 1024 | bytes 8192 | tf_op jit(solution)/shard_map/pmax | solution.py:64
  538.8 3.1 fusion.51
  542.0 2.2 fusion.49
  544.1 47.1 %psum.23 = f32[8,2,64]{2,1,0:T(2,128)S(1)} all-reduce(f32[8,2,64]{2,1,0:T(2,128)S(1)} %fusion.49), channel_id=1, replica_groups=mesh['dp'=2,'seq'=32,'tensor'=8] {'seq'}, use_global_device_ids=true, to_apply=%region_5.0 | all-reduce | flops 1024 | bytes 8192 | tf_op jit(solution)/shard_map/psum | solution.py:73
  591.3 161.5 %all-reduce.6.cloned.1.call-done = f32[8,2,64,128]{3,2,1,0:T(8,128)} async-done(((f32[8,2,64,128]{3,2,1,0:T(8,128)}), f32[8,2,64,128]{3,2,1,0:T(8,128)}) %all-reduce.6.cloned.1.call-update) | async-done | bytes 524304 | tf_op jit(solution)/shard_map/psum | solution.py:73
  754.0 7.3 pad_maximum_fusion
  761.3 2.6 copy.98
  764.0 13.2 %gather_fusion.1 = bf16[192,2,64,128]{3,2,1,0:T(8,128)(2,1)} fusion(bf16[32,9,2,64,128]{4,3,2,1,0:T(8,128)(2,1)} %all-to-all-done.1, s32[192]{0:T(256)S(1)} %bitcast.210), kind=kCustom, calls=%fused_computation.1 | custom fusion | bytes 12584448 | tf_op jit(solution)/shard_map/gather | solution.py:92
  777.1 62.3 %while.13 = (s32[]{:T(128)}, bf16[8,8,64,128]{3,2,1,0:T(8,128)(2,1)S(1)}, s32[8]{0:T(128)S(1)}, bf16[8,8,64,128]{3,2,1,0:T(8,128)(2,1)}, bf16[8,2,14,64,128]{4,3...) while((s32[]{:T(128)}, ...), condition=%wide.region_11.12_spmd.clone, body=%wide.region_8.11_spmd.clone.sunk | while | flops 205782320 | bytes 16598532 | solution.py:136
  781.3 1.5 select_reduce_fusion.2
  789.1 1.5 select_reduce_fusion.2
  796.9 1.5 select_reduce_fusion.2
  804.6 1.5 select_reduce_fusion.2
  812.4 1.5 select_reduce_fusion.2
  820.2 1.5 select_reduce_fusion.2
  828.0 1.5 select_reduce_fusion.2
  835.8 1.5 select_reduce_fusion.2
  839.6 1.7 copy.108
  (189 shorter events, 59.4 us)
Async XLA Ops:
  6.5 30.5 %copy-start.1 = (bf16[512,8,128]{2,1,0:T(8,128)(2,1)S(1)}, bf16[512,8,128]{2,1,0:T(8,128)(2,1)}, u32[]{:S(2)}) copy-start(bf16[512,8,128]{2,1,0:T(8,128)(2,1)} %param.10) | copy-start | bytes 3145732
  6.5 30.7 %copy-start = (bf16[512,8,128]{2,1,0:T(8,128)(2,1)S(1)}, bf16[512,8,128]{2,1,0:T(8,128)(2,1)}, u32[]{:S(2)}) copy-start(bf16[512,8,128]{2,1,0:T(8,128)(2,1)} %param.11) | copy-start | bytes 3145732
  20.2 28.5 %all-to-all-start = ((s32[32,1,9]{2,1,0:T(1,128)}), s32[32,1,9]{2,1,0:T(1,128)S(1)}, u32[]{:S(2)}, u32[]{:S(2)}) async-start(s32[32,1,9]{2,1,0:T(1,128)} %copy.106), calls=%async_computation | async-start | bytes 32768 | tf_op jit(solution)/shard_map/all_to_all | solution.py:84
  68.4 6.0 copy-start.2
  68.4 695.5 %all-to-all-start.1 = ((bf16[32,9,2,64,128]{4,3,2,1,0:T(8,128)(2,1)}), bf16[32,9,2,64,128]{4,3,2,1,0:T(8,128)(2,1)}, u32[]{:S(2)}, u32[]{:S(2)}) async-start(bf16[32,9,2,64,128]{4,3,2,1,0:T(8,128)(2,1)} %bitcast.199), calls=%async_computation.1 | async-start | bytes 18874368 | tf_op jit(solution)/shard_map/all_to_all | solution.py:85
  74.3 2.9 copy-start.3
  74.3 325.4 %all-reduce.4.cloned.1.call-start = ((), (), s32[]{:S(2)}) async-start(), calls=%async_computation.2 | async-start | bytes 1572864 | tf_op jit(solution)/shard_map/psum | solution.py:56
  74.4 4.3 copy-start.5
  82.5 670.2 %all-reduce.6.cloned.1.call-start = ((), (), s32[]{:S(2)}) async-start(), calls=%async_computation.3 | async-start | bytes 1048576 | tf_op jit(solution)/shard_map/psum | solution.py:73
  83.9 670.1 %collective-permute-start = (bf16[2,192,8,128]{3,2,1,0:T(8,128)(2,1)}, bf16[2,192,8,128]{3,2,1,0:T(8,128)(2,1)}, u32[]{:S(2)}, u32[]{:S(2)}) collective-permute-start(bf16[2,192,8,128]{3,2,1,0:T(8,128)(2,1)} %get-tuple-element.192), channel_id=1, source_target_pairs={{0,8},{8,16},{16,24},{24,32},{32,40},{40,48},{48,56},{56,64},{64,7... | collective-permute-start | bytes 2359304 | tf_op jit(solution)/shard_map/ppermute | solution.py:20
  87.5 666.6 %collective-permute-start.1 = (bf16[2,192,8,128]{3,2,1,0:T(8,128)(2,1)}, bf16[2,192,8,128]{3,2,1,0:T(8,128)(2,1)}, u32[]{:S(2)}, u32[]{:S(2)}) collective-permute-start(bf16[2,192,8,128]{3,2,1,0:T(8,128)(2,1)} %get-tuple-element.193), channel_id=1, source_target_pairs={{8,0},{16,8},{24,16},{32,24},{40,32},{48,40},{56,48},{64,56},{72,6... | collective-permute-start | bytes 2359304 | tf_op jit(solution)/shard_map/ppermute | solution.py:23
  764.0 13.2 %copy-start.4 = (bf16[8,8,64,128]{3,2,1,0:T(8,128)(2,1)S(1)}, bf16[8,8,64,128]{3,2,1,0:T(8,128)(2,1)}, u32[]{:S(2)}) copy-start(bf16[8,8,64,128]{3,2,1,0:T(8,128)(2,1)} %custom-call.7) | copy-start | bytes 3145732
  764.0 13.2 %copy-start.6 = (s32[8]{0:T(128)S(1)}, s32[8]{0:T(128)}, u32[]{:S(2)}) copy-start(s32[8]{0:T(128)} %param.12) | copy-start | bytes 100
Sparse Core Ops, SparseCore 0:
  82.7 317.0 all-reduce.3
  542.1 210.5 all-reduce.5
where the time goes:
time: 850 us; the launch traced here: 848 us
  waiting for transfers between devices  480 us (56%)
  blocking collectives  182 us (21%)
  local copies, waits for them, and re-layouts  85.8 us (10%)
  matrix products  30.6 us (4%)
  starting transfers between devices  28.2 us (3%)
  other arithmetic  26.6 us (3%)
  between operations  13.7 us (2%)
    psum x1, waiting for transfers between devices, local(): summed = lax.psum(picked.astype(jnp.bfloat16), 'seq')  307 us
    psum x1, waiting for transfers between devices, local(): lax.psum((local_total, local_weighted), 'seq')  161 us
    pmax x1, blocking collectives, local(): global_peak = lax.pmax(local_peak, 'seq')  135 us
    psum x1, blocking collectives, local(): lax.psum((local_total, local_weighted), 'seq')  47.1 us
    gather x1, local copies, waits for them, and re-layouts, local(): flat_pairs[wanted % local_blocks, wanted // local_blocks]  19.6 us
  transfers between devices with their start and end apart: 6, of which 3 were waited for; matrix products, arithmetic and copies ran while one was open for 4% of the time, Pallas kernels for 0%

commit v1 on v0

v1 whole, which is shorter than its diff:
```python
import math

import jax
import jax.numpy as jnp
from jax import lax
from jax.experimental import pallas as pl
from jax.experimental.pallas import tpu as pltpu
from jax.sharding import PartitionSpec as P

BLOCK = 64
WIN = 3
G = 2
R = 3
NB_DEV = 8
HEADS = 8
WIDTH = 128
SPAN = (NB_DEV + 2 * WIN) * BLOCK
WKEYS = (2 * WIN + 1) * BLOCK
FETCH = G + NB_DEV * R


def attend_kernel(spot, info, query, key_run, value_run, pool, out, fetched, sems):
    head = pl.program_id(0)

    def copies(which, slot):
        for i in range(FETCH):
            yield pltpu.make_async_copy(
                pool.at[spot[which * FETCH + i]], fetched.at[slot, i], sems.at[slot, i]
            )

    @pl.when(head == 0)
    def _():
        for copy in copies(0, 0):
            copy.start()

    @pl.when(head + 1 < HEADS)
    def _():
        for copy in copies(head + 1, (head + 1) % 2):
            copy.start()

    slot = head % 2
    for copy in copies(head, slot):
        copy.wait()
    radius = info[head]
    first = info[HEADS]
    total = info[HEADS + 1]
    column = lax.broadcasted_iota(jnp.int32, (1, WKEYS), 1) // BLOCK - WIN

    def one_block(b, carry):
        rows = pl.ds(pl.multiple_of(b * BLOCK, BLOCK), BLOCK)
        span = pl.ds(pl.multiple_of(b * BLOCK, BLOCK), WKEYS)
        q = query[0, rows]
        others = [0, 1] + [G + b * R + r for r in range(R)]
        far_keys = jnp.concatenate([fetched[slot, i, 0] for i in others], axis=0)
        far_values = jnp.concatenate([fetched[slot, i, 1] for i in others], axis=0)
        target = first + b + column
        usable = (jnp.abs(column) <= radius) & (target >= 0) & (target < total)
        contract = (((1,), (1,)), ((), ()))
        scale = 1.0 / math.sqrt(WIDTH)
        near = lax.dot_general(
            q, key_run[0, span], contract, preferred_element_type=jnp.float32
        )
        near = jnp.where(usable, near * scale, -jnp.inf)
        far = lax.dot_general(q, far_keys, contract, preferred_element_type=jnp.float32) * scale
        peak = jnp.maximum(
            jnp.max(near, axis=1, keepdims=True), jnp.max(far, axis=1, keepdims=True)
        )
        near = jnp.exp(near - peak)
        far = jnp.exp(far - peak)
        row_total = jnp.sum(near, axis=1, keepdims=True) + jnp.sum(far, axis=1, keepdims=True)
        weighted = jnp.dot(
            near.astype(jnp.bfloat16), value_run[0, span], preferred_element_type=jnp.float32
        ) + jnp.dot(far.astype(jnp.bfloat16), far_values, preferred_element_type=jnp.float32)
        out[0, rows] = (weighted / row_total).astype(jnp.bfloat16)
        return carry

    lax.fori_loop(0, NB_DEV, one_block, 0, unroll=2)


def attend(spot, info, query, key_run, value_run, pool):
    per_head = lambda rows: pl.BlockSpec((1, rows, WIDTH), lambda h, *_: (h, 0, 0))
    return pl.pallas_call(
        attend_kernel,
        grid_spec=pltpu.PrefetchScalarGridSpec(
            num_scalar_prefetch=2,
            grid=(HEADS,),
            in_specs=[
                per_head(NB_DEV * BLOCK),
                per_head(SPAN),
                per_head(SPAN),
                pl.BlockSpec(memory_space=pl.ANY),
            ],
            out_specs=per_head(NB_DEV * BLOCK),
            scratch_shapes=[
                pltpu.VMEM((2, FETCH, 2, BLOCK, WIDTH), jnp.bfloat16),
                pltpu.SemaphoreType.DMA((2, FETCH)),
            ],
        ),
        out_shape=jax.ShapeDtypeStruct((HEADS, NB_DEV * BLOCK, WIDTH), jnp.bfloat16),
        compiler_params=pltpu.CompilerParams(vmem_limit_bytes=32 * 1024 * 1024),
        name="attend",
    )(spot, info, query, key_run, value_run, pool)


def with_halo(block, width):
    count = lax.axis_size("seq")
    forward = [(i, i + 1) for i in range(count - 1)]
    backward = [(target, source) for source, target in forward]
    low = lax.ppermute(block[:, :, -width:], "seq", forward)
    high = lax.ppermute(block[:, :, :width], "seq", backward)
    return jnp.concatenate([low, block, high], axis=2)


def local(queries, keys, values, window_radius, global_ids, rand_owner, rand_local):
    shards = lax.axis_size("seq")
    position = lax.axis_index("seq")
    score_scale = 1.0 / math.sqrt(WIDTH)
    block_ids = position * NB_DEV + jnp.arange(NB_DEV, dtype=jnp.int32)

    by_head = jnp.stack((keys, values)).transpose(0, 2, 1, 3)
    pairs = by_head.reshape(2, HEADS, NB_DEV, BLOCK, WIDTH).transpose(1, 2, 0, 3, 4)
    pairs = pairs.reshape(HEADS * NB_DEV, 2, BLOCK, WIDTH)
    runs = with_halo(by_head, WIN * BLOCK)
    query_heads = queries.transpose(1, 0, 2)
    pool = lax.all_gather(pairs, "seq", axis=0, tiled=True)

    blocks_query = queries.reshape(NB_DEV, BLOCK * HEADS * WIDTH)
    selector = (global_ids[:, None] == block_ids[None, :]).astype(jnp.bfloat16)
    picked = jnp.einsum("gb,bf->gf", selector, blocks_query, preferred_element_type=jnp.float32)
    global_query = lax.psum(picked.astype(jnp.bfloat16), "seq").reshape(G, BLOCK, HEADS, WIDTH)
    global_scores = (
        jnp.einsum("gthd,hsd->hgts", global_query, by_head[0], preferred_element_type=jnp.float32)
        * score_scale
    )
    global_peak = lax.pmax(jnp.max(global_scores, axis=-1), "seq")
    global_weights = jnp.exp(global_scores - global_peak[..., None])
    local_total = jnp.sum(global_weights, axis=-1)
    local_weighted = jnp.einsum(
        "hgts,hsd->hgtd",
        global_weights.astype(jnp.bfloat16),
        by_head[1],
        preferred_element_type=jnp.float32,
    )
    global_total, global_weighted = lax.psum((local_total, local_weighted), "seq")
    global_out = (global_weighted / global_total[..., None]).astype(jnp.bfloat16)

    heads = jnp.arange(HEADS, dtype=jnp.int32)
    random_spot = rand_owner[0] * (HEADS * NB_DEV) + heads[None, :, None] * NB_DEV + rand_local[0]
    random_spot = random_spot.transpose(1, 0, 2).reshape(HEADS, NB_DEV * R)
    global_spot = (
        (global_ids // NB_DEV)[None, :] * (HEADS * NB_DEV)
        + heads[:, None] * NB_DEV
        + (global_ids % NB_DEV)[None, :]
    )
    spot = jnp.concatenate((global_spot, random_spot), axis=1).reshape(-1)
    info = jnp.concatenate(
        (window_radius, jnp.stack((position * NB_DEV, jnp.int32(shards * NB_DEV))))
    ).astype(jnp.int32)
    sparse = attend(spot, info, query_heads, runs[0], runs[1], pool)

    result = sparse.reshape(HEADS, NB_DEV, BLOCK, WIDTH).transpose(1, 2, 0, 3)
    for slot in range(G):
        owned = global_ids[slot] == block_ids
        result = jnp.where(
            owned[:, None, None, None], global_out[:, slot].transpose(1, 0, 2)[None], result
        )
    return result.reshape(NB_DEV * BLOCK, HEADS, WIDTH)


def solution(mesh):
    placed = (
        P(("dp", "seq"), "tensor", None),
        P(("dp", "seq"), "tensor", None),
        P(("dp", "seq"), "tensor", None),
        P(("dp", "tensor")),
        P("dp"),
        P("tensor", ("dp", "seq"), None, None),
        P("tensor", ("dp", "seq"), None, None),
    )
    return jax.shard_map(
        local,
        mesh=mesh,
        in_specs=placed,
        out_specs=P(("dp", "seq"), "tensor", None),
        check_vma=False,
    )
```

time: 850 us -> 884 us (1.040)
  waiting for transfers between devices: 480 us -> 715 us
  blocking collectives: 182 us -> 92.3 us
  local copies, waits for them, and re-layouts: 85.8 us -> 13.1 us
  Pallas kernels: 0 us -> 28 us
  matrix products: 30.6 us -> 6.2 us
  starting transfers between devices: 28.2 us -> 7.75 us
  other arithmetic: 26.6 us -> 8.06 us
    all_gather x0 -> x1, waiting for transfers between devices: none -> 358 us  [local(): pool = lax.all_gather(pairs, 'seq', axis=0, tiled=True)]
    psum x1, waiting for transfers between devices: 307 us -> 210 us  [local(): lax.psum(picked.astype(jnp.bfloat16), 'seq').reshape(G, BLOCK, HEADS, WIDTH)]
    pmax x1, blocking collectives: 135 us -> 46.6 us  [local(): global_peak = lax.pmax(jnp.max(global_scores, axis=-1), 'seq')]
    gather x2 -> x0, local copies, waits for them, and re-layouts: 32.7 us -> none  [the longest x1 19.6 us: local(): flat_pairs[wanted % local_blocks, wanted // local_blocks]]
    pallas_call x0 -> x1, Pallas kernels: none -> 28 us  [attend(): pl.pallas_call(attend_kernel, grid_spec=pltpu.PrefetchScalarGridSpec(num_...]
    dot_general x19 -> x3, matrix products: 30.6 us -> 6.2 us  [the longest x1 2.96 us: local(): jnp.einsum('hgts,hsd->hgtd', global_weights.astype(jnp.bfloat16), by_head...]
    all_to_all x2 -> x0, starting transfers between devices: 22.6 us -> none  [the longest x1 16.7 us: local(): lax.all_to_all(requested, 'seq', split_axis=0, concat_axis=0, tiled=True)]
    psum x1, waiting for transfers between devices: 161 us -> 147 us  [local(): lax.psum((local_total, local_weighted), 'seq')]
  transfers between devices with their start and end apart: 6 -> 5, of which waited for: 3 -> 3; matrix products, arithmetic and copies ran while one was open for 4% -> 2% of each run, Pallas kernels for 0% -> 0%
where the time goes in v1:
time: 884 us; the launch traced here: 883 us
  waiting for transfers between devices  715 us (81%)
  blocking collectives  92.3 us (10%)
  Pallas kernels  28 us (3%)
  between operations  13.4 us (2%)
  local copies, waits for them, and re-layouts  13.1 us (1%)
    all_gather x1, waiting for transfers between devices, local(): pool = lax.all_gather(pairs, 'seq', axis=0, tiled=True)  358 us
    psum x1, waiting for transfers between devices, local(): lax.psum(picked.astype(jnp.bfloat16), 'seq').reshape(G, BLOCK, HEADS, WIDTH)  210 us
    psum x1, waiting for transfers between devices, local(): lax.psum((local_total, local_weighted), 'seq')  147 us
    pmax x1, blocking collectives, local(): global_peak = lax.pmax(jnp.max(global_scores, axis=-1), 'seq')  46.6 us
    psum x1, blocking collectives, local(): lax.psum((local_total, local_weighted), 'seq')  45.6 us
    pallas_call x1, Pallas kernels, attend(): pl.pallas_call(attend_kernel, grid_spec=pltpu.PrefetchScalarGridSpec(num_...  28 us
  transfers between devices with their start and end apart: 5, of which 3 were waited for; matrix products, arithmetic and copies ran while one was open for 2% of the time, Pallas kernels for 0%

profile of v1, /device:TPU:1, one launch (start us, length us, event | category | flops | bytes accessed | tf_op | source)
XLA Modules:
  0.0 883.5 jit_solution(12331863205597402058)
XLA Ops:
  6.6 1.8 reshape.56
  8.4 0.5 fusion.2
  8.9 0.8 copy.29
  9.8 0.4 copy_bitcast_fusion.1
  10.2 1.6 pad_maximum_fusion.1
  11.8 209.6 %all-reduce.3.cloned.1.call-done = bf16[2,64,8,128]{3,1,0,2:T(8,128)(2,1)} async-done(((bf16[2,64,8,128]{3,1,0,2:T(8,128)(2,1)}), bf16[2,64,8,128]{3,1,0,2:T(8,128)(2,1)}) %all-reduce.3.cloned.1.call-update) | async-done | bytes 262160 | tf_op jit(solution)/shard_map/psum | solution.py:130
  221.4 2.8 multiply_reduce_fusion
  224.1 46.6 %pmax.7 = f32[8,2,64]{2,1,0:T(2,128)S(1)} all-reduce(f32[8,2,64]{2,1,0:T(2,128)S(1)} %get-tuple-element.17), channel_id=1, replica_groups=mesh['dp'=2,'seq'=32,'tensor'=8] {'seq'}, use_global_device_ids=true, to_apply=%region_2.0 | all-reduce | flops 1024 | bytes 8192 | tf_op jit(solution)/shard_map/pmax | solution.py:135
  270.8 3.0 fusion.3
  273.8 3.2 copy.35
  277.0 1.3 fusion.15
  278.3 3.6 collective-permute-start
  281.9 4.0 collective-permute-start.1
  286.0 0.1 copy.44
  286.2 0.1 copy.33
  286.3 0.1 add_add_fusion
  286.4 0.1 pad_add_fusion
  286.5 0.1 reshape.59.spot
  286.5 0.6 fusion.16
  287.1 1.1 broadcast_compare_fusion
  288.3 0.1 pad_add_fusion.1.info
  288.3 2.2 fusion
  290.5 45.6 %psum.23 = f32[8,2,64]{2,1,0:T(2,128)S(1)} all-reduce(f32[8,2,64]{2,1,0:T(2,128)S(1)} %fusion), channel_id=1, replica_groups=mesh['dp'=2,'seq'=32,'tensor'=8] {'seq'}, use_global_device_ids=true, to_apply=%region_5.0 | all-reduce | flops 1024 | bytes 8192 | tf_op jit(solution)/shard_map/psum | solution.py:144
  336.1 147.0 %all-reduce.5.cloned.1.call-done = f32[8,2,64,128]{3,2,1,0:T(8,128)} async-done(((f32[8,2,64,128]{3,2,1,0:T(8,128)}), f32[8,2,64,128]{3,2,1,0:T(8,128)}) %all-reduce.5.cloned.1.call-update) | async-done | bytes 524304 | tf_op jit(solution)/shard_map/psum | solution.py:144
  483.2 1.2 divide_convert_fusion
  484.5 1.5 pad_maximum_fusion
  486.0 1.5 slice_bitcast_fusion
  487.5 358.0 %all-gather.2.cloned.1.call-done.pool = bf16[2048,2,64,128]{3,2,1,0:T(8,128)(2,1)} async-done(((bf16[64,2,64,128]{3,2,1,0:T(8,128)(2,1)}), bf16[2048,2,64,128]{3,2,1,0:T(8,128)(2,1)}) %all-gather.2.cloned.1.call-update) | async-done | bytes 67108880 | tf_op jit(solution)/shard_map/all_gather | solution.py:125
  845.5 1.5 copy-done
  847.0 28.0 %attend.1 = bf16[8,512,128]{2,1,0:T(8,128)(2,1)S(1)} custom-call(s32[208]{0:T(256)S(1)} %reshape.59.spot, s32[10]{0:T(128)S(1)} %pad_add_fusion.1.info, bf16[8,512,128]{2,1,0:T(8,128)(2,1)S(1)} %bitcast.67, bf16[8,896,128]{2,1,0:T(8,128)(2,1)S(1)} %copy-done, bf16[8,896,128]{2,1,0:T(8,128)(2,1)S(1)} %get-tuple-element.5.value_run, ...), custom_call_target="tpu_custom_call" | custom-call | tf_op jit(solution)/shard_map/attend/pallas_call | solution.py:82
  875.1 0.2 select_select_fusion
  875.3 1.7 copy.36
  (31 shorter events, 0.3 us)
Async XLA Ops:
  6.5 1.8 copy-start.6
  6.5 214.8 %all-reduce.3.cloned.1.call-start = ((), (), s32[]{:S(2)}) async-start(), calls=%async_computation | async-start | bytes 524288 | tf_op jit(solution)/shard_map/psum | solution.py:130
  6.5 3.2 copy-start.2
  6.5 3.2 copy-start.3
  9.7 473.5 %all-reduce.5.cloned.1.call-start = ((), (), s32[]{:S(2)}) async-start(), calls=%async_computation.1 | async-start | bytes 1048576 | tf_op jit(solution)/shard_map/psum | solution.py:144
  273.8 571.8 %all-gather.2.cloned.1.call-start = ((), (), s32[]{:S(2)}) async-start(), calls=%async_computation.2 | async-start | bytes 69206016 | tf_op jit(solution)/shard_map/all_gather | solution.py:125
  277.0 9.0 %copy-start.1 = (bf16[512,8,128]{2,1,0:T(8,128)(2,1)S(1)}, bf16[512,8,128]{2,1,0:T(8,128)(2,1)}, u32[]{:S(2)}) copy-start(bf16[512,8,128]{2,1,0:T(8,128)(2,1)} %param.7) | copy-start | bytes 3145732
  277.0 9.1 %copy-start.4 = (s32[1,8,8,3]{2,1,3,0:T(8,128)S(1)}, s32[1,8,8,3]{2,1,3,0:T(8,128)}, u32[]{:S(2)}) copy-start(s32[1,8,8,3]{2,1,3,0:T(8,128)} %param.13) | copy-start | bytes 2308
  277.0 9.1 %copy-start.5 = (s32[1,8,8,3]{2,1,3,0:T(8,128)S(1)}, s32[1,8,8,3]{2,1,3,0:T(8,128)}, u32[]{:S(2)}) copy-start(s32[1,8,8,3]{2,1,3,0:T(8,128)} %param.12) | copy-start | bytes 2308
  277.0 11.2 %copy-start.7 = (s32[8]{0:T(128)S(1)}, s32[8]{0:T(128)}, u32[]{:S(2)}) copy-start(s32[8]{0:T(128)} %param.10) | copy-start | bytes 100
  278.3 206.1 %collective-permute-start = (bf16[2,8,192,128]{3,2,1,0:T(8,128)(2,1)}, bf16[2,8,192,128]{3,2,1,0:T(8,128)(2,1)}, u32[]{:S(2)}, u32[]{:S(2)}) collective-permute-start(bf16[2,8,192,128]{3,2,1,0:T(8,128)(2,1)} %get-tuple-element.9), channel_id=1, source_target_pairs={{0,8},{8,16},{16,24},{24,32},{32,40},{40,48},{48,56},{56,64},{64,7... | collective-permute-start | bytes 2359304 | tf_op jit(solution)/shard_map/ppermute | solution.py:109
  281.9 202.5 %collective-permute-start.1 = (bf16[2,8,192,128]{3,2,1,0:T(8,128)(2,1)}, bf16[2,8,192,128]{3,2,1,0:T(8,128)(2,1)}, u32[]{:S(2)}, u32[]{:S(2)}) collective-permute-start(bf16[2,8,192,128]{3,2,1,0:T(8,128)(2,1)} %get-tuple-element.10), channel_id=1, source_target_pairs={{8,0},{16,8},{24,16},{32,24},{40,32},{48,40},{56,48},{64,56},{72,6... | collective-permute-start | bytes 2359304 | tf_op jit(solution)/shard_map/ppermute | solution.py:110
  845.5 1.5 copy-start
Sparse Core Ops, SparseCore 0:
  9.8 211.5 all-reduce.2
  273.9 209.2 all-reduce.4
  485.3 360.1 all-gather.1

commit v2 on v1

v2 whole, which is shorter than its diff:
```python
import math

import jax
import jax.numpy as jnp
from jax import lax
from jax.experimental import pallas as pl
from jax.experimental.pallas import tpu as pltpu
from jax.sharding import PartitionSpec as P

BLOCK = 64
WIN = 3
G = 2
R = 3
NB_DEV = 8
HEADS = 8
WIDTH = 128
SPAN = (NB_DEV + 2 * WIN) * BLOCK
WKEYS = (2 * WIN + 1) * BLOCK
PICKS = NB_DEV * R
FETCH = G + PICKS

RUNS = 32
CHIPS = 16
OWN = HEADS * NB_DEV
QUNITS = 8
UNITS = 2 * QUNITS + 2 * OWN
SLOTS = 8
PHASES = 37
PIECES = 4
PIECE = SLOTS // PIECES
STAGES = 4
ENTRIES = 2 * PHASES * 2 * SLOTS
UNIT = (2, BLOCK, WIDTH)
MESH = pl.DeviceIdType.MESH


def place(seq):
    return (lax.axis_index("dp"), seq, lax.axis_index("tensor"))


def greet(devices):
    barrier = pltpu.get_barrier_semaphore()
    for device in devices:
        pl.semaphore_signal(barrier, inc=1, device_id=device, device_id_type=MESH)
    pl.semaphore_wait(barrier, len(devices))


def exchange_kernel(wanted, pairs, units, table, pool, send, land, own_sem, pair_send, pair_land):
    me = lax.axis_index("seq")
    side = lax.rem(me, 2)
    sibling = me + 1 - 2 * side
    peers = [lax.rem(me + k, RUNS) for k in range(1, RUNS)]
    greet([place(peer) for peer in peers])
    parts = (
        (units, lambda who: pl.ds(who * QUNITS, QUNITS)),
        (pairs, lambda who: pl.ds(2 * QUNITS + who * OWN, OWN)),
    )

    def across(i, who):
        source, rows = parts[i]
        return pltpu.make_async_remote_copy(
            src_ref=source,
            dst_ref=pool.at[rows(who)],
            send_sem=pair_send.at[i],
            recv_sem=pair_land.at[i],
            device_id=place(sibling),
            device_id_type=MESH,
        )

    def tell(k, slot):
        return pltpu.make_async_remote_copy(
            src_ref=wanted,
            dst_ref=table.at[slot],
            send_sem=send.at[k],
            recv_sem=land.at[k],
            device_id=place(lax.rem(me + k, RUNS)),
            device_id_type=MESH,
        )

    for k in range(1, RUNS):
        tell(k, me).start()
    kept = [pltpu.make_async_copy(wanted, table.at[me], own_sem.at[2])]
    for i in range(2):
        across(i, side).start()
        kept.append(pltpu.make_async_copy(parts[i][0], pool.at[parts[i][1](side)], own_sem.at[i]))
    for copy in kept:
        copy.start()
    for k in range(1, RUNS):
        tell(k, me).wait_send()
        tell(k, lax.rem(me + RUNS - k, RUNS)).wait_recv()
    for i in range(2):
        across(i, side).wait_send()
        across(i, 1 - side).wait_recv()
    for copy in kept:
        copy.wait()


def exchange(wanted, pairs, units):
    dma = pltpu.SemaphoreType.DMA
    return pl.pallas_call(
        exchange_kernel,
        in_specs=[
            pl.BlockSpec(memory_space=pltpu.VMEM),
            pl.BlockSpec(memory_space=pl.ANY),
            pl.BlockSpec(memory_space=pl.ANY),
        ],
        out_specs=(
            pl.BlockSpec(memory_space=pltpu.VMEM),
            pl.BlockSpec(memory_space=pl.ANY),
        ),
        out_shape=(
            jax.ShapeDtypeStruct((RUNS, HEADS, WIDTH), jnp.int32),
            jax.ShapeDtypeStruct((UNITS,) + UNIT, jnp.bfloat16),
        ),
        scratch_shapes=[
            dma((RUNS,)),
            dma((RUNS,)),
            dma((3,)),
            dma((2,)),
            dma((2,)),
        ],
        compiler_params=pltpu.CompilerParams(collective_id=0, has_side_effects=True),
        name="exchange",
    )(wanted, pairs, units)


def schedule_kernel(counts, taken, landed, rest):
    lane = lax.broadcasted_iota(jnp.int32, (2 * SLOTS, 128), 1)
    row = lax.broadcasted_iota(jnp.int32, (2 * SLOTS, 128), 0)
    wrap = lane % CHIPS == 0
    reach = [jnp.broadcast_to(counts[p : p + 1, :], (2 * SLOTS, 128)) for p in range(8)]

    def shift(x):
        return jnp.where(wrap, pltpu.roll(x, 128 - CHIPS + 1, 1), pltpu.roll(x, 1, 1))

    def phase(t, state):
        left, code, queue = state
        free = left == 0
        running = free.astype(jnp.int32)
        for step in (1, 2, 4, 8):
            running = running + jnp.where(row >= step, pltpu.roll(running, step, 0), 0)
        number = queue + running - free.astype(jnp.int32)
        fresh = free & (number < reach[0])
        extent = sum((number < reach[p]).astype(jnp.int32) for p in range(8))
        left = jnp.where(fresh, extent, left)
        code = jnp.where(fresh, lane * 256 + number, code)
        taken[t] = jnp.where(fresh, number, -1)
        used = jnp.sum(free.astype(jnp.int32), axis=0, keepdims=True)
        queue = jnp.minimum(queue + used, reach[0])
        left = shift(left)
        code = shift(code)
        landed[t] = jnp.where(left > 0, code, -1)
        return jnp.maximum(left - 1, 0), code, queue

    zero = jnp.zeros((2 * SLOTS, 128), jnp.int32)
    left, code, queue = lax.fori_loop(0, PHASES, phase, (zero, zero, zero))
    rest[...] = left + reach[0] - queue


def schedule(counts):
    return pl.pallas_call(
        schedule_kernel,
        out_shape=(
            jax.ShapeDtypeStruct((PHASES, 2 * SLOTS, 128), jnp.int32),
            jax.ShapeDtypeStruct((PHASES, 2 * SLOTS, 128), jnp.int32),
            jax.ShapeDtypeStruct((2 * SLOTS, 128), jnp.int32),
        ),
        name="schedule",
    )(counts)


def plan(table, global_ids):
    position = lax.axis_index("seq")
    chip, side = position // 2, position % 2
    codes = jnp.arange(RUNS * NB_DEV, dtype=jnp.int32)
    hit = jnp.any(table[:, :, :PICKS, None] == codes, axis=2)
    everywhere = jnp.any(codes[None, :] == global_ids[:, None], axis=0)
    hit = hit | everywhere
    delta = (jnp.arange(RUNS, dtype=jnp.int32)[:, None] // 2 - codes[None, :] // 16) & (CHIPS - 1)
    delta = delta[:, None, :]
    right = jnp.max(jnp.where(hit & (delta < 8), delta, 0), axis=0)
    left = jnp.max(jnp.where(hit & (delta > 8), CHIPS - delta, 0), axis=0)
    far = jnp.any(hit & (delta == 8), axis=0)
    even = (jnp.arange(HEADS, dtype=jnp.int32)[:, None] + codes[None, :]) % 2 == 0
    by_right = (right > left) | ((right == left) & even)
    extent = jnp.stack((jnp.where(far & by_right, 8, right), jnp.where(far & ~by_right, 8, left)))
    extent = extent.reshape(2, HEADS, CHIPS, 2, NB_DEV).transpose(0, 2, 3, 1, 4)
    extent = extent.reshape(2, CHIPS, 2 * OWN)
    holder = jnp.arange(RUNS, dtype=jnp.int32).reshape(CHIPS, 2, 1)
    unit_holder = jnp.repeat(global_ids // NB_DEV, QUNITS // G)
    query_extent = jnp.where(holder == unit_holder, 8, 0).reshape(CHIPS, 2 * QUNITS)
    extent = jnp.concatenate((jnp.stack((query_extent,) * 2), extent), axis=2)
    index = jnp.arange(UNITS, dtype=jnp.int32)
    ahead = (extent[:, :, None, :] > extent[:, :, :, None]) | (
        (extent[:, :, None, :] == extent[:, :, :, None]) & (index[None, :] < index[:, None])
    )
    rank = jnp.sum(ahead.astype(jnp.int32), axis=3)
    reach = jnp.arange(1, 9, dtype=jnp.int32)[:, None, None, None]
    counts = jnp.sum((extent[None] >= reach).astype(jnp.int32), axis=3)
    counts = jnp.concatenate((counts[:, 0], counts[:, 1, ::-1]), axis=1)
    counts = jnp.pad(counts, ((0, 0), (0, 128 - 2 * CHIPS)))
    taken, landed, rest = schedule(counts)

    def mine(x):
        pick = lambda lane: lax.dynamic_index_in_dim(x, lane, axis=2, keepdims=False)
        both = jnp.stack((pick(chip), pick(2 * CHIPS - 1 - chip)))
        return both.reshape(2, PHASES, SLOTS, 2).transpose(0, 1, 3, 2)

    own_rank = lax.dynamic_index_in_dim(rank, chip, axis=1, keepdims=False)
    own_taken = lax.dynamic_index_in_dim(mine(taken), side, axis=2, keepdims=False)
    same = own_rank[:, None, None, :] == own_taken[..., None]
    source = jnp.sum(jnp.where(same, index + 1, 0), axis=3) - 1
    arrived = mine(landed).reshape(2, 1, 1, ENTRIES // 2)
    chips = jnp.arange(CHIPS, dtype=jnp.int32)
    origin = jnp.stack((chips, 2 * CHIPS - 1 - chips))
    token = origin[:, :, None] * 256 + rank
    entry = jnp.arange(ENTRIES, dtype=jnp.int32).reshape(2, 1, 1, ENTRIES // 2)
    where = jnp.max(jnp.where(token[..., None] == arrived, entry, 0), axis=(0, 3))
    where = jnp.where((chips == chip)[:, None], ENTRIES + index[None, :], where)
    return source.reshape(-1), where.reshape(-1), rest


def packet_kernel(
    source, pool, rest, log, flag, recv, stage, votes,
    send_sem, land_sem, keep_sem, across_sem, across_land, tail_sem, vote_send, vote_land,
):
    me = lax.axis_index("seq")
    chip, side = me // 2, lax.rem(me, 2)
    sibling = me + 1 - 2 * side
    ahead = lax.rem(chip + 1, CHIPS) * 2 + side
    behind = lax.rem(chip + CHIPS - 1, CHIPS) * 2 + side
    dp, tensor = lax.axis_index("dp"), lax.axis_index("tensor")
    ring = dp * 8 + tensor

    def other(k):
        there = lax.rem(ring + k, 16)
        return (there // 8, me, lax.rem(there, 8))

    greet([place(ahead), place(behind), place(sibling)] + [other(k) for k in range(1, 16)])

    def vote(k, slot):
        return pltpu.make_async_remote_copy(
            src_ref=rest,
            dst_ref=votes.at[slot],
            send_sem=vote_send.at[k],
            recv_sem=vote_land.at[k],
            device_id=other(k),
            device_id_type=MESH,
        )

    for k in range(1, 16):
        vote(k, ring).start()
    tail = pltpu.make_async_copy(pool, log.at[pl.ds(ENTRIES, UNITS)], tail_sem.at[0])
    tail.start()
    own_vote = pltpu.make_async_copy(rest, votes.at[ring], tail_sem.at[1])
    own_vote.start()

    def hop(t, way, piece):
        rows = pl.ds(piece * PIECE, PIECE)
        return pltpu.make_async_remote_copy(
            src_ref=stage.at[way, lax.rem(t, STAGES), rows],
            dst_ref=recv.at[way, t, rows],
            send_sem=send_sem.at[way, lax.rem(t, STAGES), piece],
            recv_sem=land_sem.at[way, t, piece],
            device_id=place(ahead if way == 0 else behind),
            device_id_type=MESH,
        )

    def entry(t, way, piece, who):
        return pl.ds(((way * PHASES + t) * 2 + who) * SLOTS + piece * PIECE, PIECE)

    def keep(t, way, piece):
        return pltpu.make_async_copy(
            recv.at[way, t, pl.ds(piece * PIECE, PIECE)],
            log.at[entry(t, way, piece, side)],
            keep_sem.at[way, lax.rem(t, 2), piece],
        )

    def across(t, way, piece, who):
        return pltpu.make_async_remote_copy(
            src_ref=recv.at[way, t, pl.ds(piece * PIECE, PIECE)],
            dst_ref=log.at[entry(t, way, piece, who)],
            send_sem=across_sem.at[way, lax.rem(t, 2), piece],
            recv_sem=across_land.at[way, t, piece],
            device_id=place(sibling),
            device_id_type=MESH,
        )

    def compose(t, way, piece, first):
        for i in range(PIECE):
            slot = piece * PIECE + i
            wanted = source[(way * PHASES + t) * SLOTS + slot]
            unit = pool[jnp.maximum(wanted, 0)]
            if not first:
                unit = jnp.where(wanted >= 0, unit, recv[way, t - 1, slot])
            stage[way, lax.rem(t, STAGES), slot] = unit

    for piece in range(PIECES):
        for way in range(2):
            compose(0, way, piece, True)
            hop(0, way, piece).start()

    def arrive(t, way, piece):
        hop(t, way, piece).wait_recv()

        def settle():
            keep(t - 2, way, piece).wait()
            across(t - 2, way, piece, side).wait_send()

        pl.when(t >= 2)(settle)

    def pass_on(t, way, piece):
        keep(t, way, piece).start()
        across(t, way, piece, side).start()

    def phase(t, carry):
        def step(piece, inner):
            for way in range(2):
                arrive(t - 1, way, piece)
                pl.when(t >= STAGES)(lambda: hop(t - STAGES, way, piece).wait_send())
                compose(t, way, piece, False)
                hop(t, way, piece).start()
                pass_on(t - 1, way, piece)
            return inner

        return lax.fori_loop(0, PIECES, step, carry)

    lax.fori_loop(1, PHASES, phase, 0)

    def last(piece, carry):
        for way in range(2):
            arrive(PHASES - 1, way, piece)
            pass_on(PHASES - 1, way, piece)
            for t in range(PHASES - STAGES, PHASES):
                hop(t, way, piece).wait_send()
            for t in (PHASES - 2, PHASES - 1):
                keep(t, way, piece).wait()
                across(t, way, piece, side).wait_send()
        return carry

    lax.fori_loop(0, PIECES, last, 0)

    def drain(t, carry):
        def step(piece, inner):
            for way in range(2):
                across(t, way, piece, 1 - side).wait_recv()
            return inner

        return lax.fori_loop(0, PIECES, step, carry)

    lax.fori_loop(0, PHASES, drain, 0)
    for k in range(1, 16):
        vote(k, ring).wait_send()
        vote(k, lax.rem(ring + 16 - k, 16)).wait_recv()
    tail.wait()
    own_vote.wait()
    flag[...] = jnp.max(votes[...], axis=0)


def packets(source, pool, rest):
    dma = pltpu.SemaphoreType.DMA
    vmem = pl.BlockSpec(memory_space=pltpu.VMEM)
    return pl.pallas_call(
        packet_kernel,
        in_specs=[pl.BlockSpec(memory_space=pltpu.SMEM), vmem, vmem],
        out_specs=(pl.BlockSpec(memory_space=pl.ANY), vmem),
        out_shape=(
            jax.ShapeDtypeStruct((ENTRIES + UNITS,) + UNIT, jnp.bfloat16),
            jax.ShapeDtypeStruct((2 * SLOTS, 128), jnp.int32),
        ),
        scratch_shapes=[
            pltpu.VMEM((2, PHASES, SLOTS) + UNIT, jnp.bfloat16),
            pltpu.VMEM((2, STAGES, SLOTS) + UNIT, jnp.bfloat16),
            pltpu.VMEM((16, 2 * SLOTS, 128), jnp.int32),
            dma((2, STAGES, PIECES)),
            dma((2, PHASES, PIECES)),
            dma((2, 2, PIECES)),
            dma((2, 2, PIECES)),
            dma((2, PHASES, PIECES)),
            dma((2,)),
            dma((16,)),
            dma((16,)),
        ],
        compiler_params=pltpu.CompilerParams(
            collective_id=1, has_side_effects=True, vmem_limit_bytes=48 * 1024 * 1024
        ),
        name="packets",
    )(source, pool, rest)


def attend_kernel(
    fast, where, wanted, info, query, key_run, value_run, pool, query_pool, out, part, stats,
    fetched, asked, sems, asked_sems,
):
    head = pl.program_id(0)

    def spot(code, h):
        low = code & (NB_DEV - 1)
        if fast:
            inner = 2 * QUNITS + ((code >> 3) & 1) * OWN + h * NB_DEV + low
            return where[(code >> 4) * UNITS + inner]
        return (code >> 3) * OWN + h * NB_DEV + low

    def query_spot(g, h):
        unit = g * (QUNITS // G) + h // 2
        if fast:
            code = info[HEADS + 2 + g]
            return where[(code >> 4) * UNITS + ((code >> 3) & 1) * QUNITS + unit]
        return unit

    def copies(h, slot):
        for i in range(FETCH):
            code = info[HEADS + 2 + i] if i < G else wanted[h * PICKS + i - G]
            yield pltpu.make_async_copy(
                pool.at[spot(code, h)], fetched.at[slot, i], sems.at[slot, i]
            )
        for g in range(G):
            yield pltpu.make_async_copy(
                query_pool.at[query_spot(g, h), h % 2], asked.at[slot, g], asked_sems.at[slot, g]
            )

    @pl.when(head == 0)
    def _():
        for copy in copies(head, 0):
            copy.start()

    @pl.when(head + 1 < HEADS)
    def _():
        for copy in copies(head + 1, (head + 1) % 2):
            copy.start()

    slot = head % 2
    for copy in copies(head, slot):
        copy.wait()
    radius = info[head]
    first = info[HEADS]
    total = info[HEADS + 1]
    column = lax.broadcasted_iota(jnp.int32, (1, WKEYS), 1) // BLOCK - WIN
    contract = (((1,), (1,)), ((), ()))
    scale = 1.0 / math.sqrt(WIDTH)

    own = pl.ds(WIN * BLOCK, NB_DEV * BLOCK)
    scores = scale * lax.dot_general(
        key_run[0, own],
        asked[slot].reshape(G * BLOCK, WIDTH),
        contract,
        preferred_element_type=jnp.float32,
    )
    peak = jnp.max(scores, axis=0, keepdims=True)
    weights = jnp.exp(scores - peak)
    sums = jnp.sum(weights, axis=0, keepdims=True)
    weighted = lax.dot_general(
        value_run[0, own],
        weights.astype(jnp.bfloat16),
        (((0,), (0,)), ((), ())),
        preferred_element_type=jnp.float32,
    )
    part[0] = (weighted / sums).astype(jnp.bfloat16)
    stats[0] = jnp.concatenate((peak, sums, jnp.zeros((6, WIDTH), jnp.float32)), axis=0)

    def one_block(b, carry):
        rows = pl.ds(pl.multiple_of(b * BLOCK, BLOCK), BLOCK)
        span = pl.ds(pl.multiple_of(b * BLOCK, BLOCK), WKEYS)
        q = query[0, rows]
        others = [0, 1] + [G + b * R + r for r in range(R)]
        far_keys = jnp.concatenate([fetched[slot, i, 0] for i in others], axis=0)
        far_values = jnp.concatenate([fetched[slot, i, 1] for i in others], axis=0)
        target = first + b + column
        usable = (jnp.abs(column) <= radius) & (target >= 0) & (target < total)
        near = lax.dot_general(
            q, key_run[0, span], contract, preferred_element_type=jnp.float32
        )
        near = jnp.where(usable, near * scale, -jnp.inf)
        far = lax.dot_general(q, far_keys, contract, preferred_element_type=jnp.float32) * scale
        peak = jnp.maximum(
            jnp.max(near, axis=1, keepdims=True), jnp.max(far, axis=1, keepdims=True)
        )
        near = jnp.exp(near - peak)
        far = jnp.exp(far - peak)
        row_total = jnp.sum(near, axis=1, keepdims=True) + jnp.sum(far, axis=1, keepdims=True)
        weighted = jnp.dot(
            near.astype(jnp.bfloat16), value_run[0, span], preferred_element_type=jnp.float32
        ) + jnp.dot(far.astype(jnp.bfloat16), far_values, preferred_element_type=jnp.float32)
        out[0, rows] = (weighted / row_total).astype(jnp.bfloat16)
        return carry

    lax.fori_loop(0, NB_DEV, one_block, 0, unroll=2)


def attend(fast, where, wanted, info, query, key_run, value_run, pool, query_pool):
    per_head = lambda rows: pl.BlockSpec((1, rows, WIDTH), lambda h, *_: (h, 0, 0))
    return pl.pallas_call(
        lambda *refs: attend_kernel(fast, *refs),
        grid_spec=pltpu.PrefetchScalarGridSpec(
            num_scalar_prefetch=3,
            grid=(HEADS,),
            in_specs=[
                per_head(NB_DEV * BLOCK),
                per_head(SPAN),
                per_head(SPAN),
                pl.BlockSpec(memory_space=pl.ANY),
                pl.BlockSpec(memory_space=pl.ANY),
            ],
            out_specs=(per_head(NB_DEV * BLOCK), per_head(WIDTH), per_head(8)),
            scratch_shapes=[
                pltpu.VMEM((2, FETCH) + UNIT, jnp.bfloat16),
                pltpu.VMEM((2, G, BLOCK, WIDTH), jnp.bfloat16),
                pltpu.SemaphoreType.DMA((2, FETCH)),
                pltpu.SemaphoreType.DMA((2, G)),
            ],
        ),
        out_shape=(
            jax.ShapeDtypeStruct((HEADS, NB_DEV * BLOCK, WIDTH), jnp.bfloat16),
            jax.ShapeDtypeStruct((HEADS, WIDTH, G * BLOCK), jnp.bfloat16),
            jax.ShapeDtypeStruct((HEADS, 8, G * BLOCK), jnp.float32),
        ),
        compiler_params=pltpu.CompilerParams(vmem_limit_bytes=32 * 1024 * 1024),
        name="attend" if fast else "attend_gathered",
    )(where, wanted, info, query, key_run, value_run, pool, query_pool)


SHARE = HEADS * WIDTH // RUNS


def merge_kernel(part, stats, merged, got, got_stats, piece, send, land, send_stats, land_stats, back, home):
    me = lax.axis_index("seq")
    peers = [lax.rem(me + k, RUNS) for k in range(1, RUNS)]
    greet([place(peer) for peer in peers])

    def rows(who):
        return who // 4, pl.ds(lax.rem(who, 4) * SHARE, SHARE)

    def hand(k, slot):
        to = lax.rem(me + k, RUNS)
        head, span = rows(to)
        weighted = pltpu.make_async_remote_copy(
            src_ref=part.at[head, span],
            dst_ref=got.at[slot],
            send_sem=send.at[k],
            recv_sem=land.at[k],
            device_id=place(to),
            device_id_type=MESH,
        )
        sums = pltpu.make_async_remote_copy(
            src_ref=stats.at[head],
            dst_ref=got_stats.at[slot],
            send_sem=send_stats.at[k],
            recv_sem=land_stats.at[k],
            device_id=place(to),
            device_id_type=MESH,
        )
        return weighted, sums

    def give(k, who):
        head, span = rows(who)
        return pltpu.make_async_remote_copy(
            src_ref=piece,
            dst_ref=merged.at[head, span],
            send_sem=back.at[k],
            recv_sem=home.at[k],
            device_id=place(lax.rem(me + k, RUNS)),
            device_id_type=MESH,
        )

    for k in range(1, RUNS):
        for copy in hand(k, me):
            copy.start()
    head, span = rows(me)
    got[me] = part[head, span]
    got_stats[me] = stats[head]
    for k in range(1, RUNS):
        for copy in hand(k, lax.rem(me + RUNS - k, RUNS)):
            copy.wait_recv()
    peaks = got_stats[:, 0, :]
    weights = got_stats[:, 1, :] * jnp.exp(peaks - jnp.max(peaks, axis=0, keepdims=True))
    weights = weights / jnp.sum(weights, axis=0, keepdims=True)
    total = jnp.zeros((SHARE, G * BLOCK), jnp.float32)
    for device in range(RUNS):
        total = total + weights[device : device + 1, :] * got[device].astype(jnp.float32)
    piece[...] = total.astype(jnp.bfloat16)
    for k in range(1, RUNS):
        give(k, me).start()
    merged[head, span] = piece[...]
    for k in range(1, RUNS):
        for copy in hand(k, me):
            copy.wait_send()
        give(k, me).wait_send()
        give(k, lax.rem(me + RUNS - k, RUNS)).wait_recv()


def merge(part, stats):
    dma = pltpu.SemaphoreType.DMA
    vmem = pl.BlockSpec(memory_space=pltpu.VMEM)
    return pl.pallas_call(
        merge_kernel,
        in_specs=[vmem, vmem],
        out_specs=vmem,
        out_shape=jax.ShapeDtypeStruct((HEADS, WIDTH, G * BLOCK), jnp.bfloat16),
        scratch_shapes=[
            pltpu.VMEM((RUNS, SHARE, G * BLOCK), jnp.bfloat16),
            pltpu.VMEM((RUNS, 8, G * BLOCK), jnp.float32),
            pltpu.VMEM((SHARE, G * BLOCK), jnp.bfloat16),
        ]
        + [dma((RUNS,))] * 6,
        compiler_params=pltpu.CompilerParams(collective_id=2, has_side_effects=True),
        name="merge",
    )(part, stats)


def with_halo(block, width):
    count = lax.axis_size("seq")
    forward = [(i, i + 1) for i in range(count - 1)]
    backward = [(target, source) for source, target in forward]
    low = lax.ppermute(block[:, :, -width:], "seq", forward)
    high = lax.ppermute(block[:, :, :width], "seq", backward)
    return jnp.concatenate([low, block, high], axis=2)


def local(queries, keys, values, window_radius, global_ids, rand_owner, rand_local):
    shards = lax.axis_size("seq")
    position = lax.axis_index("seq")
    block_ids = position * NB_DEV + jnp.arange(NB_DEV, dtype=jnp.int32)

    by_head = jnp.stack((keys, values)).transpose(0, 2, 1, 3)
    pairs = by_head.reshape(2, HEADS, NB_DEV, BLOCK, WIDTH).transpose(1, 2, 0, 3, 4)
    pairs = pairs.reshape((OWN,) + UNIT)
    query_heads = queries.transpose(1, 0, 2)
    query_blocks = query_heads.reshape(HEADS, NB_DEV, BLOCK, WIDTH)
    units = jnp.concatenate(
        [
            lax.dynamic_index_in_dim(query_blocks, global_ids[g] % NB_DEV, axis=1, keepdims=False)
            for g in range(G)
        ]
    ).reshape((QUNITS,) + UNIT)
    wanted = (rand_owner[0] * NB_DEV + rand_local[0]).astype(jnp.int32)
    wanted = wanted.transpose(1, 0, 2).reshape(HEADS, PICKS)
    table, pool = exchange(jnp.pad(wanted, ((0, 0), (0, WIDTH - PICKS))), pairs, units)
    source, where, rest = plan(table, global_ids)
    log, flag = packets(source, pool, rest)

    runs = with_halo(by_head, WIN * BLOCK)
    info = jnp.concatenate(
        (window_radius, jnp.stack((position * NB_DEV, jnp.int32(shards * NB_DEV))), global_ids)
    ).astype(jnp.int32)
    rest_args = (where, wanted.reshape(-1), info, query_heads, runs[0], runs[1])

    def from_packets(pairs, units, log):
        return attend(True, *rest_args, log, log)

    def from_gather(pairs, units, log):
        everything = lax.all_gather(pairs, "seq", axis=0, tiled=True)
        holder = jnp.repeat(global_ids // NB_DEV, QUNITS // G) == position
        asked = lax.psum(jnp.where(holder[:, None, None, None], units, 0), "seq")
        return attend(False, *rest_args, everything, asked)

    sparse, part, stats = lax.cond(
        jnp.max(flag) > 0, from_gather, from_packets, pairs, units, log
    )
    global_out = merge(part, stats).reshape(HEADS, WIDTH, G, BLOCK).transpose(2, 3, 0, 1)

    result = sparse.reshape(HEADS, NB_DEV, BLOCK, WIDTH).transpose(1, 2, 0, 3)
    for slot in range(G):
        owned = global_ids[slot] == block_ids
        result = jnp.where(owned[:, None, None, None], global_out[slot][None], result)
    return result.reshape(NB_DEV * BLOCK, HEADS, WIDTH)


def solution(mesh):
    placed = (
        P(("dp", "seq"), "tensor", None),
        P(("dp", "seq"), "tensor", None),
        P(("dp", "seq"), "tensor", None),
        P(("dp", "tensor")),
        P("dp"),
        P("tensor", ("dp", "seq"), None, None),
        P("tensor", ("dp", "seq"), None, None),
    )
    return jax.shard_map(
        local,
        mesh=mesh,
        in_specs=placed,
        out_specs=P(("dp", "seq"), "tensor", None),
        check_vma=False,
    )
```

time: 884 us -> 428 us (0.48)
  waiting for transfers between devices: 715 us -> 0.01 us
  Pallas kernels: 28 us -> 333 us
  blocking collectives: 92.3 us -> 0 us
  other arithmetic: 8.06 us -> 33.3 us
  local copies, waits for them, and re-layouts: 13.1 us -> 30.6 us
    all_gather x1 -> x0, waiting for transfers between devices: 358 us -> none  [local(): pool = lax.all_gather(pairs, 'seq', axis=0, tiled=True)]
    psum x2 -> x0, waiting for transfers between devices: 357 us -> none  [the longest x1 210 us: local(): lax.psum(picked.astype(jnp.bfloat16), 'seq').reshape(G, BLOCK, HEADS, WIDTH)]
    pallas_call x1 -> x5, Pallas kernels: 28 us -> 333 us  [the longest x1 229 us: packets(): pl.pallas_call(packet_kernel, in_specs=[pl.BlockSpec(memory_space=pltpu.S...]
    pmax x1 -> x0, blocking collectives: 46.6 us -> none  [local(): global_peak = lax.pmax(jnp.max(global_scores, axis=-1), 'seq')]
    psum x1 -> x0, blocking collectives: 45.6 us -> none  [local(): lax.psum((local_total, local_weighted), 'seq')]
    dynamic_slice x0 -> x7, local copies, waits for them, and re-layouts: none -> 8.96 us  [the longest x6 8.95 us: mine(): lax.dynamic_index_in_dim(x, lane, axis=2, keepdims=False)]
  transfers between devices with their start and end apart: 5 -> 2, of which waited for: 3 -> 0; matrix products, arithmetic and copies ran while one was open for 2% -> 11% of each run, Pallas kernels for 0% -> 60%
where the time goes in v2:
time: 428 us; the launch traced here: 426 us
  Pallas kernels  333 us (78%)
  other arithmetic  33.3 us (8%)
  local copies, waits for them, and re-layouts  30.6 us (7%)
  between operations  18.1 us (4%)
  starting transfers between devices  11 us (3%)
    pallas_call x1, Pallas kernels, packets(): pl.pallas_call(packet_kernel, in_specs=[pl.BlockSpec(memory_space=pltpu.S...  229 us
    pallas_call x1, Pallas kernels, merge(): pl.pallas_call(merge_kernel, in_specs=[vmem, vmem], out_specs=vmem, out_s...  44.6 us
    pallas_call x1, Pallas kernels, attend(): pl.pallas_call(lambda *refs: attend_kernel(fast, *refs), grid_spec=pltpu....  33.4 us
    pallas_call x1, Pallas kernels, exchange(): pl.pallas_call(exchange_kernel, in_specs=[pl.BlockSpec(memory_space=pltpu...  21.3 us
    dynamic_slice x6, local copies, waits for them, and re-layouts, mine(): lax.dynamic_index_in_dim(x, lane, axis=2, keepdims=False)  8.95 us
  transfers between devices with their start and end apart: 2, of which 0 were waited for; matrix products, arithmetic and copies ran while one was open for 11% of the time, Pallas kernels for 60%

profile of v2, /device:TPU:1, one launch (start us, length us, event | category | flops | bytes accessed | tf_op | source)
XLA Modules:
  0.0 426.4 jit_solution(16385946672849546768)
XLA Ops:
  6.5 1.9 copy_bitcast_fusion
  8.5 1.6 fusion.18
  10.1 1.4 copy-done.4
  11.5 1.3 fusion.20
  12.8 4.9 %collective-permute-start = (bf16[2,8,192,128]{3,2,1,0:T(8,128)(2,1)}, bf16[2,8,192,128]{3,2,1,0:T(8,128)(2,1)}, u32[]{:S(2)}, u32[]{:S(2)}) collective-permute-start(bf16[2,8,192,128]{3,2,1,0:T(8,128)(2,1)} %get-tuple-element.82), channel_id=1, source_target_pairs={{0,8},{8,16},{16,24},{24,32},{32,40},{40,48},{48,56},{56,64},{64,7... | collective-permute-start | bytes 2359304 | tf_op jit(solution)/shard_map/ppermute | solution.py:614
  17.8 6.1 %collective-permute-start.1 = (bf16[2,8,192,128]{3,2,1,0:T(8,128)(2,1)}, bf16[2,8,192,128]{3,2,1,0:T(8,128)(2,1)}, u32[]{:S(2)}, u32[]{:S(2)}) collective-permute-start(bf16[2,8,192,128]{3,2,1,0:T(8,128)(2,1)} %get-tuple-element.83), channel_id=1, source_target_pairs={{8,0},{16,8},{24,16},{32,24},{40,32},{48,40},{56,48},{64,56},{72,6... | collective-permute-start | bytes 2359304 | tf_op jit(solution)/shard_map/ppermute | solution.py:615
  36.3 1.8 copy.73
  38.2 21.3 %exchange.1 = (s32[32,8,128]{2,1,0:T(8,128)}, bf16[144,2,64,128]{3,2,1,0:T(8,128)(2,1)}) custom-call(s32[8,128]{1,0:T(8,128)} %pad.8.wanted, bf16[64,2,64,128]{3,2,1,0:T(8,128)(2,1)S(1)} %bitcast.72, bf16[8,2,64,128]{3,2,1,0:T(8,128)(2,1)S(1)} %bitcast.78), custom_call_target="tpu_custom_call" | custom-call | tf_op jit(solution)/shard_map/exchange/pallas_call | solution.py:100
  59.5 2.9 fusion.1
  62.5 1.4 and_reduce_fusion
  63.8 1.4 copy.75
  65.2 1.5 select_reduce_fusion.3
  66.7 1.5 copy.96
  73.6 3.3 convert_reduce_fusion
  79.5 5.0 %schedule.1 = (s32[37,16,128]{2,1,0:T(8,128)}, s32[37,16,128]{2,1,0:T(8,128)}, s32[16,128]{1,0:T(8,128)}) custom-call(s32[8,128]{1,0:T(8,128)} %pad.9.counts), custom_call_target="tpu_custom_call" | custom-call | tf_op jit(solution)/shard_map/schedule/pallas_call | solution.py:161
  84.5 2.1 constant_dynamic-slice_fusion.2
  86.6 1.2 copy.86
  87.7 1.2 copy.85
  89.0 2.0 select_reduce_fusion.1
  91.2 2.2 constant_dynamic-slice_fusion.1
  93.3 1.2 copy.88
  94.5 1.2 copy.89
  96.0 2.6 select_reduce_fusion
  99.4 2.3 copy-done
  101.7 229.0 %packets.1 = (bf16[1328,2,64,128]{3,2,1,0:T(8,128)(2,1)}, s32[16,128]{1,0:T(8,128)S(1)}) custom-call(s32[592]{0:T(1024)S(1)} %sub.136.source, bf16[144,2,64,128]{3,2,1,0:T(8,128)(2,1)S(1)} %copy-done, s32[16,128]{1,0:T(8,128)S(1)} %copy-done.2), custom_call_target="tpu_custom_call" | custom-call | tf_op jit(solution)/shard_map/packets/pallas_call | solution.py:363
  332.8 1.2 fusion.16
  334.0 2.1 pad_maximum_fusion
  336.2 2.2 slice_bitcast_fusion
  338.3 33.6 %conditional.1 = ((bf16[8,512,128]{2,1,0:T(8,128)(2,1)S(1)}, bf16[8,128,128]{2,1,0:T(8,128)(2,1)S(1)}, f32[8,8,128]{2,1,0:T(8,128)S(1)})) conditional(s32[]{:T(128)} %convert_element_type.13, (s32[2304]{0:T(1024)S(1)}, s32[192]{0:T(256)S(1)}, s32[12]{0:T(128)S(1)}, bf16[8,512,128]{2,1,0:T(8,128)(2,1)S(1)}, bf16[8,896,128]{2,1,0:T(8,128)(2,1)}, ...), branch_computations={%region_10.11_spmd, %region_11.13_spmd} | conditional | flops 262176 | bytes 219152576 | solution.py:656
  338.3 33.4 %attend.1 = (bf16[8,512,128]{2,1,0:T(8,128)(2,1)S(1)}, bf16[8,128,128]{2,1,0:T(8,128)(2,1)S(1)}, f32[8,8,128]{2,1,0:T(8,128)S(1)}) custom-call(s32[2304]{0:T(1024)S(1)} %get-tuple-element.39.refs_0_, s32[192]{0:T(256)S(1)} %get-tuple-element.40.refs_1_, s32[12]{0:T(128)S(1)} %get-tuple-element.41.refs_2_, ...), custom_call_target="tpu_custom_call" | custom-call | tf_op jit(solution)/shard_map/cond/branch_0_fun/attend/pallas_call | solution.py:492
  372.0 44.6 %merge.1 = bf16[8,128,128]{2,1,0:T(8,128)(2,1)} custom-call(bf16[8,128,128]{2,1,0:T(8,128)(2,1)S(1)} %get-tuple-element.73.part, f32[8,8,128]{2,1,0:T(8,128)S(1)} %get-tuple-element.74.stats), custom_call_target="tpu_custom_call" | custom-call | tf_op jit(solution)/shard_map/merge/pallas_call | solution.py:594
  417.9 1.6 fusion.2
  (85 shorter events, 20.9 us)
Async XLA Ops:
  8.4 16.0 %copy-start.10 = (s32[2]{0:T(128)S(1)}, s32[2]{0:T(128)}, u32[]{:S(2)}) copy-start(s32[2]{0:T(128)} %param.13) | copy-start | bytes 28
  8.5 23.7 %copy-start.7 = (s32[1,8,8,3]{2,1,3,0:T(8,128)S(1)}, s32[1,8,8,3]{2,1,3,0:T(8,128)}, u32[]{:S(2)}) copy-start(s32[1,8,8,3]{2,1,3,0:T(8,128)} %param.15) | copy-start | bytes 2308
  8.5 23.7 %copy-start.8 = (s32[1,8,8,3]{2,1,3,0:T(8,128)S(1)}, s32[1,8,8,3]{2,1,3,0:T(8,128)}, u32[]{:S(2)}) copy-start(s32[1,8,8,3]{2,1,3,0:T(8,128)} %param.14) | copy-start | bytes 2308
  8.5 27.7 %copy-start.5 = (bf16[512,8,128]{2,1,0:T(8,128)(2,1)S(1)}, bf16[512,8,128]{2,1,0:T(8,128)(2,1)}, u32[]{:S(2)}) copy-start(bf16[512,8,128]{2,1,0:T(8,128)(2,1)} %param.9) | copy-start | bytes 3145732
  10.1 1.4 copy-start.4
  12.8 321.2 %collective-permute-start = (bf16[2,8,192,128]{3,2,1,0:T(8,128)(2,1)}, bf16[2,8,192,128]{3,2,1,0:T(8,128)(2,1)}, u32[]{:S(2)}, u32[]{:S(2)}) collective-permute-start(bf16[2,8,192,128]{3,2,1,0:T(8,128)(2,1)} %get-tuple-element.82), channel_id=1, source_target_pairs={{0,8},{8,16},{16,24},{24,32},{32,40},{40,48},{48,56},{56,64},{64,7... | collective-permute-start | bytes 2359304 | tf_op jit(solution)/shard_map/ppermute | solution.py:614
  17.8 316.2 %collective-permute-start.1 = (bf16[2,8,192,128]{3,2,1,0:T(8,128)(2,1)}, bf16[2,8,192,128]{3,2,1,0:T(8,128)(2,1)}, u32[]{:S(2)}, u32[]{:S(2)}) collective-permute-start(bf16[2,8,192,128]{3,2,1,0:T(8,128)(2,1)} %get-tuple-element.83), channel_id=1, source_target_pairs={{8,0},{16,8},{24,16},{32,24},{40,32},{48,40},{56,48},{64,56},{72,6... | collective-permute-start | bytes 2359304 | tf_op jit(solution)/shard_map/ppermute | solution.py:615
  73.5 22.4 %copy-start.6 = (s32[2,592]{1,0:T(2,128)S(1)}, s32[2,592]{1,0:T(2,128)}, u32[]{:S(2)}) copy-start(s32[2,592]{1,0:T(2,128)} %multiply_add_fusion.1) | copy-start | bytes 14212
  84.5 14.9 %copy-start.2 = (s32[16,128]{1,0:T(8,128)S(1)}, s32[16,128]{1,0:T(8,128)}, u32[]{:S(2)}) copy-start(s32[16,128]{1,0:T(8,128)} %get-tuple-element.69.rest) | copy-start | bytes 24580
  99.4 2.3 copy-start
  336.1 2.2 copy-start.9
  336.2 2.2 copy-start.11

commit v3 on v2

v3 whole, which is shorter than its diff:
```python
import math

import jax
import jax.numpy as jnp
from jax import lax
from jax.experimental import pallas as pl
from jax.experimental.pallas import tpu as pltpu
from jax.sharding import PartitionSpec as P

BLOCK = 64
WIN = 3
G = 2
R = 3
NB_DEV = 8
HEADS = 8
WIDTH = 128
WKEYS = (2 * WIN + 1) * BLOCK
PICKS = NB_DEV * R
NEAR = NB_DEV + 2 * WIN
FETCH = NEAR + G + PICKS

RUNS = 32
CHIPS = 16
CODES = RUNS * NB_DEV
OWN = HEADS * NB_DEV
QUNITS = 8
UNITS = 2 * QUNITS + 2 * OWN
SLOTS = 8
PHASES = 37
PIECES = 4
PIECE = SLOTS // PIECES
STAGES = 4
ENTRIES = 2 * PHASES * 2 * SLOTS
UNIT = (2, BLOCK, WIDTH)
MESH = pl.DeviceIdType.MESH


def place(seq):
    return (lax.axis_index("dp"), seq, lax.axis_index("tensor"))


def greet(devices):
    barrier = pltpu.get_barrier_semaphore()
    for device in devices:
        pl.semaphore_signal(barrier, inc=1, device_id=device, device_id_type=MESH)
    pl.semaphore_wait(barrier, len(devices))


def exchange_kernel(wanted, pairs, units, table, pool, send, land, kept_sem, pair_send, pair_land):
    me = lax.axis_index("seq")
    side = lax.rem(me, 2)
    greet([place(lax.rem(me + k, RUNS)) for k in range(1, RUNS)])
    parts = (
        (units, lambda who: pool.at[pl.ds(who * QUNITS, QUNITS)]),
        (pairs, lambda who: pool.at[pl.ds(2 * QUNITS + who * OWN, OWN)]),
    )

    def across(i, who):
        return pltpu.make_async_remote_copy(
            src_ref=parts[i][0],
            dst_ref=parts[i][1](who),
            send_sem=pair_send.at[i],
            recv_sem=pair_land.at[i],
            device_id=place(me + 1 - 2 * side),
            device_id_type=MESH,
        )

    def tell(k, slot):
        return pltpu.make_async_remote_copy(
            src_ref=wanted,
            dst_ref=table.at[slot],
            send_sem=send.at[k],
            recv_sem=land.at[k],
            device_id=place(lax.rem(me + k, RUNS)),
            device_id_type=MESH,
        )

    for k in range(1, RUNS):
        tell(k, me).start()
    kept = [pltpu.make_async_copy(wanted, table.at[me], kept_sem.at[2])]
    for i in range(2):
        across(i, side).start()
        kept.append(pltpu.make_async_copy(parts[i][0], parts[i][1](side), kept_sem.at[i]))
    for copy in kept:
        copy.start()
    for k in range(1, RUNS):
        tell(k, me).wait_send()
        tell(k, lax.rem(me + RUNS - k, RUNS)).wait_recv()
    for i in range(2):
        across(i, side).wait_send()
        across(i, 1 - side).wait_recv()
    for copy in kept:
        copy.wait()


def exchange(wanted, pairs, units):
    dma = pltpu.SemaphoreType.DMA
    vmem = pl.BlockSpec(memory_space=pltpu.VMEM)
    hbm = pl.BlockSpec(memory_space=pl.ANY)
    return pl.pallas_call(
        exchange_kernel,
        in_specs=[vmem, hbm, hbm],
        out_specs=(vmem, hbm),
        out_shape=(
            jax.ShapeDtypeStruct((RUNS, HEADS, WIDTH), jnp.int32),
            jax.ShapeDtypeStruct((UNITS,) + UNIT, jnp.bfloat16),
        ),
        scratch_shapes=[dma((RUNS,)), dma((RUNS,)), dma((3,)), dma((2,)), dma((2,))],
        compiler_params=pltpu.CompilerParams(collective_id=0, has_side_effects=True),
        name="exchange",
    )(wanted, pairs, units)


def plan_kernel(global_ids, table, radius, source, where, rest, keys, numbers, sems):
    me = lax.axis_index("seq")
    chip, side = me // 2, lax.rem(me, 2)
    shape = (HEADS, CODES)
    code = lax.broadcasted_iota(jnp.int32, shape, 1)
    row = lax.broadcasted_iota(jnp.int32, shape, 0)
    home = code >> 4
    first, second = global_ids[0], global_ids[1]
    everywhere = ((code == first) | (code == second)).astype(jnp.int32)

    def reaches(d, state):
        right, left, far = state
        picked = table[d]
        apart = code - d * NB_DEV
        beside = (apart >= -radius[...]) & (apart < NB_DEV + radius[...])
        hit = everywhere | beside.astype(jnp.int32)
        for k in range(PICKS):
            hit = hit | (picked[:, k : k + 1] == code).astype(jnp.int32)
        delta = ((d >> 1) - home) & (CHIPS - 1)
        right = jnp.maximum(right, jnp.where(delta < 8, hit * delta, 0))
        left = jnp.maximum(left, jnp.where(delta > 8, hit * (CHIPS - delta), 0))
        return right, left, far | jnp.where(delta == 8, hit, 0)

    zero = jnp.zeros(shape, jnp.int32)
    right, left, far = lax.fori_loop(0, RUNS, reaches, (zero, zero, zero))
    by_right = (right > left) | ((right == left) & (((row + code) & 1) == 0))
    right = jnp.where((far > 0) & by_right, 8, right)
    left = jnp.where((far > 0) & ~by_right, 8, left)

    lane_i = lax.broadcasted_iota(jnp.int32, (CODES, CODES), 0)
    lane_j = lax.broadcasted_iota(jnp.int32, (CODES, CODES), 1)
    together = (lane_i >> 4) == (lane_j >> 4)
    group = together.astype(jnp.bfloat16)
    before = (together & (lane_i < lane_j)).astype(jnp.bfloat16)
    holds_first = (home == (first >> 4)).astype(jnp.int32)
    holds_second = (home == (second >> 4)).astype(jnp.int32)
    asked = (holds_first + holds_second) * (QUNITS // G)

    def running_rows(x):
        height = x.shape[0]
        line = lax.broadcasted_iota(jnp.int32, x.shape, 0)
        step = 1
        while step < height:
            x = x + jnp.where(line >= step, pltpu.roll(x, step, 0), 0)
            step *= 2
        return x

    def last_row(x):
        return jnp.broadcast_to(x[x.shape[0] - 1 :, :], x.shape)

    def order(extent):
        rank = jnp.full(shape, 4096, jnp.int32)
        reach = [None] * 9
        above = asked
        for p in range(8, 0, -1):
            same = (extent == p).astype(jnp.bfloat16)
            in_group = jnp.dot(same, group, preferred_element_type=jnp.float32).astype(jnp.int32)
            ahead = jnp.dot(same, before, preferred_element_type=jnp.float32).astype(jnp.int32)
            running = running_rows(in_group)
            rank = jnp.where(extent == p, above + running - in_group + ahead, rank)
            above = above + last_row(running)
            reach[p] = above
        return rank, reach

    ways = [order(extent) for extent in (right, left)]
    wide = lambda x: jnp.concatenate((x, x), axis=0)
    reaches_wide = [[None] + [wide(x) for x in reach[1:]] for rank, reach in ways]

    def phase(t, state):
        after = []
        for way in range(2):
            rank, reach = ways[way][0], reaches_wide[way]
            going, queue, start, slot = state[4 * way : 4 * way + 4]
            free = (going == 0).astype(jnp.int32)
            running = running_rows(free)
            nth = running - free
            number = queue + nth
            fresh = (free > 0) & (number < reach[1])
            extent = sum((number < reach[p]).astype(jnp.int32) for p in range(1, 9))
            going = jnp.where(fresh, extent, going)
            taken = jnp.minimum(queue + last_row(running), reach[1])
            mark = jnp.where(fresh, number, -1)
            for s in range(2 * SLOTS):
                here = rank == jnp.broadcast_to(mark[s : s + 1, :], shape)
                start = jnp.where(here, t, start)
                slot = jnp.where(here, s, slot)
            going = jnp.maximum(pltpu.roll(going, 16 if way == 0 else CODES - 16, 1) - 1, 0)
            after += [going, taken, start, slot]
        return tuple(after)

    state = lax.fori_loop(0, PHASES, phase, (wide(zero), wide(zero), zero, zero) * 2)
    over = wide(zero)
    for way in range(2):
        over = over + state[4 * way] + reaches_wide[way][1] - state[4 * way + 1]
    over = over[:HEADS] + over[HEADS:]
    rest[...] = over[:, :128] + over[:, 128:]

    delta = (chip - home) & (CHIPS - 1)
    core = (code >> 3) & 1
    near = ENTRIES + 2 * QUNITS + core * OWN + row * NB_DEV + (code & 7)
    goes = [state[2] + delta - 1, PHASES + state[6] + CHIPS - delta - 1]
    slots = [state[3], state[7]]
    entry = [(goes[way] * 2 + (slots[way] & 1)) * SLOTS + (slots[way] >> 1) for way in range(2)]
    from_left = (delta < 8) | ((delta == 8) & (right == 8))
    far_entry = jnp.clip(jnp.where(from_left, entry[0], entry[1]), 0, ENTRIES - 1)
    where[...] = jnp.where(delta == 0, near, far_entry)

    for way in range(2):
        rank, reach = ways[way]
        sent = rank < state[4 * way + 1][:HEADS]
        keys[way] = jnp.where(sent, state[4 * way + 2] * 2 * SLOTS + state[4 * way + 3], -1)
    fetch = pltpu.make_async_copy(keys, numbers, sems)
    fetch.start()
    fetch.wait()

    def clear(i, carry):
        source[i] = -1
        return carry

    lax.fori_loop(0, 2 * PHASES * SLOTS, clear, 0, unroll=8)
    base = chip * 2 * NB_DEV
    has = [chip == (first >> 4), chip == (second >> 4)]
    count = (has[0].astype(jnp.int32) + has[1].astype(jnp.int32)) * (QUNITS // G)
    for way in range(2):

        def put(i, carry):
            lane = i & 15
            key = numbers[way, i >> 4, base + lane]

            @pl.when((key >= 0) & ((key & 1) == side))
            def _():
                unit = 2 * QUNITS + (lane >> 3) * OWN + (i >> 4) * NB_DEV + (lane & 7)
                source[way * PHASES * SLOTS + (key >> 1)] = unit

            return carry

        lax.fori_loop(0, 2 * OWN, put, 0, unroll=4)
        for r in range(QUNITS):
            late = jnp.logical_not(has[0]) if r < QUNITS // G else True
            late = jnp.asarray(late)
            core = (jnp.where(late, second, first) >> 3) & 1
            unit = core * QUNITS + jnp.where(late, QUNITS // G, 0) + r % (QUNITS // G)

            @pl.when((r < count) & (side == r % 2))
            def _():
                source[way * PHASES * SLOTS + r // 2] = unit


def plan(global_ids, table, radius):
    vmem = pl.BlockSpec(memory_space=pltpu.VMEM)
    smem = pl.BlockSpec(memory_space=pltpu.SMEM)
    return pl.pallas_call(
        plan_kernel,
        in_specs=[smem, vmem, vmem],
        out_specs=(smem, vmem, vmem),
        out_shape=(
            jax.ShapeDtypeStruct((2 * PHASES * SLOTS,), jnp.int32),
            jax.ShapeDtypeStruct((HEADS, CODES), jnp.int32),
            jax.ShapeDtypeStruct((HEADS, 128), jnp.int32),
        ),
        scratch_shapes=[
            pltpu.VMEM((2, HEADS, CODES), jnp.int32),
            pltpu.SMEM((2, HEADS, CODES), jnp.int32),
            pltpu.SemaphoreType.DMA(()),
        ],
        name="plan",
    )(global_ids, table, radius)


def packet_kernel(
    source, pool, rest, log, flag, recv, stage, votes,
    send_sem, land_sem, keep_sem, across_sem, across_land, tail_sem, vote_send, vote_land,
):
    me = lax.axis_index("seq")
    chip, side = me // 2, lax.rem(me, 2)
    sibling = me + 1 - 2 * side
    ahead = lax.rem(chip + 1, CHIPS) * 2 + side
    behind = lax.rem(chip + CHIPS - 1, CHIPS) * 2 + side
    dp, tensor = lax.axis_index("dp"), lax.axis_index("tensor")
    ring = dp * 8 + tensor

    def other(k):
        there = lax.rem(ring + k, 16)
        return (there // 8, me, lax.rem(there, 8))

    greet([place(ahead), place(behind), place(sibling)] + [other(k) for k in range(1, 16)])

    def vote(k, slot):
        return pltpu.make_async_remote_copy(
            src_ref=rest,
            dst_ref=votes.at[slot],
            send_sem=vote_send.at[k],
            recv_sem=vote_land.at[k],
            device_id=other(k),
            device_id_type=MESH,
        )

    for k in range(1, 16):
        vote(k, ring).start()
    kept = pltpu.make_async_copy(pool, log.at[pl.ds(ENTRIES, UNITS)], tail_sem.at[0])
    kept.start()
    own_vote = pltpu.make_async_copy(rest, votes.at[ring], tail_sem.at[1])
    own_vote.start()

    def hop(t, way, piece):
        rows = pl.ds(piece * PIECE, PIECE)
        return pltpu.make_async_remote_copy(
            src_ref=stage.at[way, lax.rem(t, STAGES), rows],
            dst_ref=recv.at[way, t, rows],
            send_sem=send_sem.at[way, lax.rem(t, STAGES), piece],
            recv_sem=land_sem.at[way, t, piece],
            device_id=place(ahead if way == 0 else behind),
            device_id_type=MESH,
        )

    def entry(t, way, who):
        return pl.ds(((way * PHASES + t) * 2 + who) * SLOTS, SLOTS)

    def keep(t, way):
        return pltpu.make_async_copy(
            recv.at[way, t], log.at[entry(t, way, side)], keep_sem.at[way, lax.rem(t, 2)]
        )

    def across(t, way, who):
        return pltpu.make_async_remote_copy(
            src_ref=recv.at[way, t],
            dst_ref=log.at[entry(t, way, who)],
            send_sem=across_sem.at[way, lax.rem(t, 2)],
            recv_sem=across_land.at[way, t],
            device_id=place(sibling),
            device_id_type=MESH,
        )

    def compose(t, way, piece, first):
        for i in range(PIECE):
            slot = piece * PIECE + i
            wanted = source[(way * PHASES + t) * SLOTS + slot]
            unit = pool[jnp.maximum(wanted, 0)]
            if not first:
                unit = jnp.where(wanted >= 0, unit, recv[way, t - 1, slot])
            stage[way, lax.rem(t, STAGES), slot] = unit

    for piece in range(PIECES):
        for way in range(2):
            compose(0, way, piece, True)
            hop(0, way, piece).start()

    def settle(t):
        for way in range(2):
            keep(t, way).wait()
            across(t, way, side).wait_send()

    def pass_on(t):
        pl.when(t >= 2)(lambda: settle(t - 2))
        for way in range(2):
            keep(t, way).start()
            across(t, way, side).start()

    def phase(t, carry):
        def step(piece, inner):
            for way in range(2):
                hop(t - 1, way, piece).wait_recv()
                pl.when(t >= STAGES)(lambda: hop(t - STAGES, way, piece).wait_send())
                compose(t, way, piece, False)
                hop(t, way, piece).start()
            return inner

        lax.fori_loop(0, PIECES, step, 0, unroll=True)
        pass_on(t - 1)
        return carry

    lax.fori_loop(1, PHASES, phase, 0)

    def last(piece, carry):
        for way in range(2):
            hop(PHASES - 1, way, piece).wait_recv()
            for t in range(PHASES - STAGES, PHASES):
                hop(t, way, piece).wait_send()
        return carry

    lax.fori_loop(0, PIECES, last, 0)
    pass_on(PHASES - 1)
    settle(PHASES - 2)
    settle(PHASES - 1)

    def drain(t, carry):
        for way in range(2):
            across(t, way, 1 - side).wait_recv()
        return carry

    lax.fori_loop(0, PHASES, drain, 0)
    for k in range(1, 16):
        vote(k, ring).wait_send()
        vote(k, lax.rem(ring + 16 - k, 16)).wait_recv()
    kept.wait()
    own_vote.wait()
    flag[...] = jnp.max(votes[...], axis=0)


def packets(source, pool, rest):
    dma = pltpu.SemaphoreType.DMA
    vmem = pl.BlockSpec(memory_space=pltpu.VMEM)
    return pl.pallas_call(
        packet_kernel,
        in_specs=[
            pl.BlockSpec(memory_space=pltpu.SMEM),
            vmem,
            vmem,
        ],
        out_specs=(pl.BlockSpec(memory_space=pl.ANY), vmem),
        out_shape=(
            jax.ShapeDtypeStruct((ENTRIES + UNITS,) + UNIT, jnp.bfloat16),
            jax.ShapeDtypeStruct((HEADS, 128), jnp.int32),
        ),
        scratch_shapes=[
            pltpu.VMEM((2, PHASES, SLOTS) + UNIT, jnp.bfloat16),
            pltpu.VMEM((2, STAGES, SLOTS) + UNIT, jnp.bfloat16),
            pltpu.VMEM((16, HEADS, 128), jnp.int32),
            dma((2, STAGES, PIECES)),
            dma((2, PHASES, PIECES)),
            dma((2, 2)),
            dma((2, 2)),
            dma((2, PHASES)),
            dma((2,)),
            dma((16,)),
            dma((16,)),
        ],
        compiler_params=pltpu.CompilerParams(
            collective_id=1, has_side_effects=True, vmem_limit_bytes=48 * 1024 * 1024
        ),
        name="packets",
    )(source, pool, rest)


def attend_kernel(
    fast, where, wanted, info, query, pool, query_pool, out, part, stats,
    fetched, asked, sems, asked_sems,
):
    head = pl.program_id(0)
    first = info[HEADS]

    def spot(code, h):
        if fast:
            return where[h, code]
        return (code >> 3) * OWN + h * NB_DEV + (code & 7)

    def query_spot(g, h):
        unit = g * (QUNITS // G) + h // 2
        if not fast:
            return unit
        mine = first >> 3
        owner = info[HEADS + 1 + g] >> 3
        core = owner & 1
        delta = ((mine >> 1) - (owner >> 1)) & (CHIPS - 1)
        shared = (owner >> 1) == (info[HEADS + 1] >> 4)
        rank = jnp.where(shared, unit, h // 2)
        near = ENTRIES + core * QUNITS + unit
        step = jnp.where(delta <= 8, delta - 1, PHASES + CHIPS - delta - 1)
        far = (step * 2 + (rank & 1)) * SLOTS + (rank >> 1)
        return jnp.where(delta == 0, near, far)

    def copies(h, slot):
        for i in range(FETCH):
            if i < NEAR:
                code = jnp.clip(first - WIN + i, 0, CODES - 1)
            elif i < NEAR + G:
                code = info[HEADS + 1 + i - NEAR]
            else:
                code = wanted[h * PICKS + i - NEAR - G]
            yield pltpu.make_async_copy(
                pool.at[spot(code, h)], fetched.at[slot, i], sems.at[slot, i]
            )
        for g in range(G):
            yield pltpu.make_async_copy(
                query_pool.at[query_spot(g, h), h % 2], asked.at[slot, g], asked_sems.at[slot, g]
            )

    @pl.when(head == 0)
    def _():
        for copy in copies(head, 0):
            copy.start()

    @pl.when(head + 1 < HEADS)
    def _():
        for copy in copies(head + 1, (head + 1) % 2):
            copy.start()

    slot = head % 2
    for copy in copies(head, slot):
        copy.wait()
    radius = info[head]
    column = lax.broadcasted_iota(jnp.int32, (1, WKEYS), 1) // BLOCK - WIN
    contract = (((1,), (1,)), ((), ()))
    scale = 1.0 / math.sqrt(WIDTH)

    own = range(WIN, WIN + NB_DEV)
    scores = scale * lax.dot_general(
        jnp.concatenate([fetched[slot, i, 0] for i in own], axis=0),
        asked[slot].reshape(G * BLOCK, WIDTH),
        contract,
        preferred_element_type=jnp.float32,
    )
    peak = jnp.max(scores, axis=0, keepdims=True)
    weights = jnp.exp(scores - peak)
    sums = jnp.sum(weights, axis=0, keepdims=True)
    weighted = lax.dot_general(
        jnp.concatenate([fetched[slot, i, 1] for i in own], axis=0),
        weights.astype(jnp.bfloat16),
        (((0,), (0,)), ((), ())),
        preferred_element_type=jnp.float32,
    )
    part[0] = (weighted / sums).astype(jnp.bfloat16)
    stats[0] = jnp.concatenate((peak, sums, jnp.zeros((6, WIDTH), jnp.float32)), axis=0)

    def one_block(b, carry):
        rows = pl.ds(pl.multiple_of(b * BLOCK, BLOCK), BLOCK)
        q = query[0, rows]
        window = [b + i for i in range(2 * WIN + 1)]
        near_keys = jnp.concatenate([fetched[slot, i, 0] for i in window], axis=0)
        near_values = jnp.concatenate([fetched[slot, i, 1] for i in window], axis=0)
        others = [NEAR, NEAR + 1] + [NEAR + G + b * R + r for r in range(R)]
        far_keys = jnp.concatenate([fetched[slot, i, 0] for i in others], axis=0)
        far_values = jnp.concatenate([fetched[slot, i, 1] for i in others], axis=0)
        target = first + b + column
        usable = (jnp.abs(column) <= radius) & (target >= 0) & (target < CODES)
        near = lax.dot_general(q, near_keys, contract, preferred_element_type=jnp.float32)
        near = jnp.where(usable, near * scale, -jnp.inf)
        far = lax.dot_general(q, far_keys, contract, preferred_element_type=jnp.float32) * scale
        peak = jnp.maximum(
            jnp.max(near, axis=1, keepdims=True), jnp.max(far, axis=1, keepdims=True)
        )
        near = jnp.exp(near - peak)
        far = jnp.exp(far - peak)
        row_total = jnp.sum(near, axis=1, keepdims=True) + jnp.sum(far, axis=1, keepdims=True)
        weighted = jnp.dot(
            near.astype(jnp.bfloat16), near_values, preferred_element_type=jnp.float32
        ) + jnp.dot(far.astype(jnp.bfloat16), far_values, preferred_element_type=jnp.float32)
        out[0, rows] = (weighted / row_total).astype(jnp.bfloat16)
        return carry

    lax.fori_loop(0, NB_DEV, one_block, 0, unroll=2)


def attend(fast, where, wanted, info, query, pool, query_pool):
    per_head = lambda rows: pl.BlockSpec((1, rows, WIDTH), lambda h, *_: (h, 0, 0))
    return pl.pallas_call(
        lambda *refs: attend_kernel(fast, *refs),
        grid_spec=pltpu.PrefetchScalarGridSpec(
            num_scalar_prefetch=3,
            grid=(HEADS,),
            in_specs=[
                per_head(NB_DEV * BLOCK),
                pl.BlockSpec(memory_space=pl.ANY),
                pl.BlockSpec(memory_space=pl.ANY),
            ],
            out_specs=(per_head(NB_DEV * BLOCK), per_head(WIDTH), per_head(8)),
            scratch_shapes=[
                pltpu.VMEM((2, FETCH) + UNIT, jnp.bfloat16),
                pltpu.VMEM((2, G, BLOCK, WIDTH), jnp.bfloat16),
                pltpu.SemaphoreType.DMA((2, FETCH)),
                pltpu.SemaphoreType.DMA((2, G)),
            ],
        ),
        out_shape=(
            jax.ShapeDtypeStruct((HEADS, NB_DEV * BLOCK, WIDTH), jnp.bfloat16),
            jax.ShapeDtypeStruct((HEADS, WIDTH, G * BLOCK), jnp.bfloat16),
            jax.ShapeDtypeStruct((HEADS, 8, G * BLOCK), jnp.float32),
        ),
        compiler_params=pltpu.CompilerParams(vmem_limit_bytes=32 * 1024 * 1024),
        name="attend" if fast else "attend_gathered",
    )(where, wanted, info, query, pool, query_pool)


HALF = HEADS // 2
SHARE = HALF * WIDTH // CHIPS


def merge_kernel(
    part, stats, merged, theirs, their_stats, half, half_stats, got, got_stats, piece,
    pair_send, pair_land, send, land, send_stats, land_stats, back, home,
):
    me = lax.axis_index("seq")
    chip, side = me // 2, lax.rem(me, 2)
    sibling = me + 1 - 2 * side
    peers = [lax.rem(chip + k, CHIPS) * 2 + side for k in range(1, CHIPS)]
    greet([place(peer) for peer in peers] + [place(sibling)])

    def pair(i, source, target):
        return pltpu.make_async_remote_copy(
            src_ref=source,
            dst_ref=target,
            send_sem=pair_send.at[i],
            recv_sem=pair_land.at[i],
            device_id=place(sibling),
            device_id_type=MESH,
        )

    their_heads = pl.ds((1 - side) * HALF, HALF)
    my_heads = pl.ds(side * HALF, HALF)
    swaps = [
        pair(0, part.at[their_heads], theirs),
        pair(1, stats.at[their_heads], their_stats),
    ]
    for copy in swaps:
        copy.start()
    for copy in swaps:
        copy.wait_recv()
    for h in range(HALF):
        mine = stats[side * HALF + h]
        other = their_stats[h]
        peak = jnp.maximum(mine[0:1, :], other[0:1, :])
        first = mine[1:2, :] * jnp.exp(mine[0:1, :] - peak)
        second = other[1:2, :] * jnp.exp(other[0:1, :] - peak)
        total = first + second
        weighted = (first / total) * part[side * HALF + h].astype(jnp.float32) + (
            second / total
        ) * theirs[h].astype(jnp.float32)
        half[h] = weighted.astype(jnp.bfloat16)
        half_stats[h : h + 1, :] = peak
        half_stats[HALF + h : HALF + h + 1, :] = total

    def rows(who):
        return who // 4, pl.ds(lax.rem(who, 4) * SHARE, SHARE)

    def hand(k, slot):
        to = lax.rem(chip + k, CHIPS)
        head, span = rows(to)
        weighted = pltpu.make_async_remote_copy(
            src_ref=half.at[head, span],
            dst_ref=got.at[slot],
            send_sem=send.at[k],
            recv_sem=land.at[k],
            device_id=place(to * 2 + side),
            device_id_type=MESH,
        )
        sums = pltpu.make_async_remote_copy(
            src_ref=half_stats,
            dst_ref=got_stats.at[slot],
            send_sem=send_stats.at[k],
            recv_sem=land_stats.at[k],
            device_id=place(to * 2 + side),
            device_id_type=MESH,
        )
        return weighted, sums

    def give(k, who):
        head, span = rows(who)
        return pltpu.make_async_remote_copy(
            src_ref=piece,
            dst_ref=merged.at[side * HALF + head, span],
            send_sem=back.at[k],
            recv_sem=home.at[k],
            device_id=place(lax.rem(chip + k, CHIPS) * 2 + side),
            device_id_type=MESH,
        )

    for k in range(1, CHIPS):
        for copy in hand(k, chip):
            copy.start()
    head, span = rows(chip)
    got[chip] = half[head, span]
    got_stats[chip] = half_stats[...]
    for k in range(1, CHIPS):
        for copy in hand(k, lax.rem(chip + CHIPS - k, CHIPS)):
            copy.wait_recv()
    all_stats = got_stats[...]
    peaks = jnp.zeros((CHIPS, G * BLOCK), jnp.float32)
    sums = jnp.zeros((CHIPS, G * BLOCK), jnp.float32)
    for h in range(HALF):
        peaks = jnp.where(head == h, all_stats[:, h, :], peaks)
        sums = jnp.where(head == h, all_stats[:, HALF + h, :], sums)
    weights = sums * jnp.exp(peaks - jnp.max(peaks, axis=0, keepdims=True))
    weights = weights / jnp.sum(weights, axis=0, keepdims=True)
    total = jnp.zeros((SHARE, G * BLOCK), jnp.float32)
    for k in range(CHIPS):
        total = total + weights[k : k + 1, :] * got[k].astype(jnp.float32)
    piece[...] = total.astype(jnp.bfloat16)
    for k in range(1, CHIPS):
        give(k, chip).start()
    merged[side * HALF + head, span] = piece[...]
    for k in range(1, CHIPS):
        give(k, lax.rem(chip + CHIPS - k, CHIPS)).wait_recv()
    last = pair(2, merged.at[my_heads], merged.at[my_heads])
    last.start()
    for copy in swaps:
        copy.wait_send()
    for k in range(1, CHIPS):
        for copy in hand(k, chip):
            copy.wait_send()
        give(k, chip).wait_send()
    last.wait_send()
    pair(2, merged.at[their_heads], merged.at[their_heads]).wait_recv()


def merge(part, stats):
    dma = pltpu.SemaphoreType.DMA
    vmem = pl.BlockSpec(memory_space=pltpu.VMEM)
    rows = G * BLOCK
    return pl.pallas_call(
        merge_kernel,
        in_specs=[vmem, vmem],
        out_specs=vmem,
        out_shape=jax.ShapeDtypeStruct((HEADS, WIDTH, rows), jnp.bfloat16),
        scratch_shapes=[
            pltpu.VMEM((HALF, WIDTH, rows), jnp.bfloat16),
            pltpu.VMEM((HALF, 8, rows), jnp.float32),
            pltpu.VMEM((HALF, WIDTH, rows), jnp.bfloat16),
            pltpu.VMEM((2 * HALF, rows), jnp.float32),
            pltpu.VMEM((CHIPS, SHARE, rows), jnp.bfloat16),
            pltpu.VMEM((CHIPS, 2 * HALF, rows), jnp.float32),
            pltpu.VMEM((SHARE, rows), jnp.bfloat16),
        ]
        + [dma((3,))] * 2
        + [dma((CHIPS,))] * 6,
        compiler_params=pltpu.CompilerParams(collective_id=2, has_side_effects=True),
        name="merge",
    )(part, stats)


def local(queries, keys, values, window_radius, global_ids, rand_owner, rand_local):
    position = lax.axis_index("seq")
    block_ids = position * NB_DEV + jnp.arange(NB_DEV, dtype=jnp.int32)

    pairs = jnp.stack((keys, values)).reshape(2, NB_DEV, BLOCK, HEADS, WIDTH)
    pairs = pairs.transpose(3, 1, 0, 2, 4).reshape((OWN,) + UNIT)
    query_heads = queries.transpose(1, 0, 2)
    query_blocks = query_heads.reshape(HEADS, NB_DEV, BLOCK, WIDTH)
    units = jnp.concatenate(
        [
            lax.dynamic_index_in_dim(query_blocks, global_ids[g] % NB_DEV, axis=1, keepdims=False)
            for g in range(G)
        ]
    ).reshape((QUNITS,) + UNIT)
    wanted = (rand_owner[0] * NB_DEV + rand_local[0]).astype(jnp.int32)
    wanted = wanted.transpose(1, 0, 2).reshape(HEADS, PICKS)
    table, pool = exchange(jnp.pad(wanted, ((0, 0), (0, WIDTH - PICKS))), pairs, units)
    radius = jnp.broadcast_to(window_radius[:, None], (HEADS, CODES)).astype(jnp.int32)
    source, where, rest = plan(global_ids, table, radius)
    log, flag = packets(source, pool, rest)
    info = jnp.concatenate((window_radius, (position * NB_DEV)[None], global_ids)).astype(jnp.int32)
    rest_args = (where, wanted.reshape(-1), info, query_heads)

    def from_packets(pairs, units, log):
        return attend(True, *rest_args, log, log)

    def from_gather(pairs, units, log):
        everything = lax.all_gather(pairs, "seq", axis=0, tiled=True)
        holder = jnp.repeat(global_ids // NB_DEV, QUNITS // G) == position
        asked = lax.psum(jnp.where(holder[:, None, None, None], units, 0), "seq")
        return attend(False, *rest_args, everything, asked)

    sparse, part, stats = lax.cond(
        jnp.max(flag) > 0, from_gather, from_packets, pairs, units, log
    )
    global_out = merge(part, stats).reshape(HEADS, WIDTH, G, BLOCK).transpose(2, 3, 0, 1)

    result = sparse.reshape(HEADS, NB_DEV, BLOCK, WIDTH).transpose(1, 2, 0, 3)
    for slot in range(G):
        owned = global_ids[slot] == block_ids
        result = jnp.where(owned[:, None, None, None], global_out[slot][None], result)
    return result.reshape(NB_DEV * BLOCK, HEADS, WIDTH)


def solution(mesh):
    placed = (
        P(("dp", "seq"), "tensor", None),
        P(("dp", "seq"), "tensor", None),
        P(("dp", "seq"), "tensor", None),
        P(("dp", "tensor")),
        P("dp"),
        P("tensor", ("dp", "seq"), None, None),
        P("tensor", ("dp", "seq"), None, None),
    )
    return jax.shard_map(
        local,
        mesh=mesh,
        in_specs=placed,
        out_specs=P(("dp", "seq"), "tensor", None),
        check_vma=False,
    )
```

time: 428 us -> 368 us (0.86)
  other arithmetic: 33.3 us -> 5.34 us
  local copies, waits for them, and re-layouts: 30.6 us -> 11.4 us
  starting transfers between devices: 11 us -> 0 us
    pallas_call x2, Pallas kernels: 26.3 us -> 41.1 us  [the longest x1 25.5 us: exchange(): pl.pallas_call(exchange_kernel, in_specs=[vmem, hbm, hbm], out_specs=(vme...]
    ppermute x2 -> x0, starting transfers between devices: 11 us -> none  [the longest x1 6.06 us: with_halo(): high = lax.ppermute(block[:, :, :width], 'seq', backward)]
    pallas_call x1, Pallas kernels: 44.6 us -> 33.9 us  [merge(): pl.pallas_call(merge_kernel, in_specs=[vmem, vmem], out_specs=vmem, out_s...]
    dynamic_slice x7 -> x0, local copies, waits for them, and re-layouts: 8.96 us -> none  [the longest x6 8.95 us: mine(): lax.dynamic_index_in_dim(x, lane, axis=2, keepdims=False)]
    reduce_sum x3 -> x0, other arithmetic: 6.41 us -> none  [the longest x1 3.3 us: plan(): rank = jnp.sum(ahead.astype(jnp.int32), axis=3)]
    reduce_or x3 -> x0, other arithmetic: 4.95 us -> none  [the longest x1 2.92 us: plan(): hit = jnp.any(table[:, :, :PICKS, None] == codes, axis=2)]
    pallas_call x1, Pallas kernels: 229 us -> 224 us  [packets(): pl.pallas_call(packet_kernel, in_specs=[pl.BlockSpec(memory_space=pltpu.S...]
  transfers between devices with their start and end apart: 2 -> 0, of which waited for: 0 -> 0; matrix products, arithmetic and copies ran while one was open for 11% -> 0% of each run, Pallas kernels for 60% -> 0%
where the time goes in v3:
time: 368 us; the launch traced here: 367 us
  Pallas kernels  332 us (90%)
  between operations  17.8 us (5%)
  local copies, waits for them, and re-layouts  11.4 us (3%)
  other arithmetic  5.34 us (1%)
    pallas_call x1, Pallas kernels, packets(): pl.pallas_call(packet_kernel, in_specs=[pl.BlockSpec(memory_space=pltpu.S...  224 us
    pallas_call x1, Pallas kernels, merge(): pl.pallas_call(merge_kernel, in_specs=[vmem, vmem], out_specs=vmem, out_s...  33.9 us
    pallas_call x1, Pallas kernels, attend(): pl.pallas_call(lambda *refs: attend_kernel(fast, *refs), grid_spec=pltpu....  33.2 us
    pallas_call x1, Pallas kernels, exchange(): pl.pallas_call(exchange_kernel, in_specs=[vmem, hbm, hbm], out_specs=(vme...  25.5 us
    pallas_call x1, Pallas kernels, plan(): pl.pallas_call(plan_kernel, in_specs=[smem, vmem, vmem], out_specs=(smem,...  15.6 us

profile of v3, /device:TPU:1, one launch (start us, length us, event | category | flops | bytes accessed | tf_op | source)
XLA Modules:
  0.0 366.9 jit_solution(17073370880517796730)
XLA Ops:
  6.5 0.8 pad_add_fusion
  7.4 1.3 fusion.5
  12.3 1.2 fusion.2
  13.6 1.3 broadcast_in_dim.58.radius
  14.9 0.7 add_bitcast_fusion
  15.6 0.1 copy.26
  15.7 0.6 pad.4.wanted
  16.3 0.1 copy.30
  16.4 0.1 reshape_reshape.3
  16.6 1.4 copy.40
  17.9 0.0 copy-start.6
  18.0 0.0 copy-done.5
  18.0 0.3 copy.27
  18.3 0.9 copy-done.6
  19.2 0.3 copy.28
  19.4 0.2 pad_maximum_fusion
  19.6 0.0 copy-start.7
  19.6 25.5 %exchange.1 = (s32[32,8,128]{2,1,0:T(8,128)}, bf16[144,2,64,128]{3,2,1,0:T(8,128)(2,1)}) custom-call(s32[8,128]{1,0:T(8,128)} %pad.4.wanted, bf16[64,2,64,128]{3,2,1,0:T(8,128)(2,1)S(1)} %bitcast.37, bf16[8,2,64,128]{3,2,1,0:T(8,128)(2,1)S(1)} %bitcast.42), custom_call_target="tpu_custom_call" | custom-call | tf_op jit(solution)/shard_map/exchange/pallas_call | solution.py:100
  45.2 0.0 copy-done.7
  45.2 15.6 %plan.1 = (s32[592]{0:T(1024)}, s32[8,256]{1,0:T(8,128)S(1)}, s32[8,128]{1,0:T(8,128)}) custom-call(s32[2]{0:T(128)S(1)} %copy-done.7, s32[32,8,128]{2,1,0:T(8,128)} %get-tuple-element.54.table, s32[8,256]{1,0:T(8,128)} %broadcast_in_dim.58.radius), custom_call_target="tpu_custom_call" | custom-call | tf_op jit(solution)/shard_map/plan/pallas_call | solution.py:265
  60.8 0.0 copy-start
  60.8 2.3 copy-done
  63.2 0.7 copy-done.2
  63.8 0.7 copy-done.3
  64.5 224.0 %packets.1 = (bf16[1328,2,64,128]{3,2,1,0:T(8,128)(2,1)}, s32[8,128]{1,0:T(8,128)S(1)}) custom-call(s32[592]{0:T(1024)S(1)} %copy-done.2, bf16[144,2,64,128]{3,2,1,0:T(8,128)(2,1)S(1)} %copy-done, s32[8,128]{1,0:T(8,128)S(1)} %copy-done.3), custom_call_target="tpu_custom_call" | custom-call | tf_op jit(solution)/shard_map/packets/pallas_call | solution.py:416
  288.6 0.6 reduce_max.9
  289.9 33.3 %conditional.1 = ((bf16[8,512,128]{2,1,0:T(8,128)(2,1)S(1)}, bf16[8,128,128]{2,1,0:T(8,128)(2,1)S(1)}, f32[8,8,128]{2,1,0:T(8,128)S(1)})) conditional(s32[]{:T(128)} %convert_element_type.5, (s32[8,256]{1,0:T(8,128)S(1)}, s32[192]{0:T(256)S(1)}, s32[11]{0:T(128)S(1)}, bf16[8,512,128]{2,1,0:T(8,128)(2,1)S(1)}, ...), branch_computations={%region_1.2_spmd, %region_2.4_spmd} | conditional | flops 262176 | bytes 219152576 | solution.py:765
  289.9 33.2 %attend.1 = (bf16[8,512,128]{2,1,0:T(8,128)(2,1)S(1)}, bf16[8,128,128]{2,1,0:T(8,128)(2,1)S(1)}, f32[8,8,128]{2,1,0:T(8,128)S(1)}) custom-call(s32[8,256]{1,0:T(8,128)S(1)} %get-tuple-element.31.refs_0_, s32[192]{0:T(256)S(1)} %get-tuple-element.32.refs_1_, s32[11]{0:T(128)S(1)} %get-tuple-element.33.refs_2_, ...), custom_call_target="tpu_custom_call" | custom-call | tf_op jit(solution)/shard_map/cond/branch_0_fun/attend/pallas_call | solution.py:559
  323.1 33.9 %merge.1 = bf16[8,128,128]{2,1,0:T(8,128)(2,1)} custom-call(bf16[8,128,128]{2,1,0:T(8,128)(2,1)S(1)} %get-tuple-element.61.part, f32[8,8,128]{2,1,0:T(8,128)S(1)} %get-tuple-element.62.stats), custom_call_target="tpu_custom_call" | custom-call | tf_op jit(solution)/shard_map/merge/pallas_call | solution.py:712
  357.0 1.1 copy.31
  358.2 0.2 copy_bitcast_fusion
  358.3 1.7 fusion.1
  (8 shorter events, 0.1 us)
Async XLA Ops:
  6.5 11.5 %copy-start.5 = (bf16[512,8,128]{2,1,0:T(8,128)(2,1)S(1)}, bf16[512,8,128]{2,1,0:T(8,128)(2,1)}, u32[]{:S(2)}) copy-start(bf16[512,8,128]{2,1,0:T(8,128)(2,1)} %param.10) | copy-start | bytes 3145732
  17.9 1.2 copy-start.6
  19.6 25.6 %copy-start.7 = (s32[2]{0:T(128)S(1)}, s32[2]{0:T(128)}, u32[]{:S(2)}) copy-start(s32[2]{0:T(128)} %global_ids.1) | copy-start | bytes 28
  60.8 2.3 copy-start
  63.2 0.7 copy-start.2
  63.8 0.7 copy-start.3

commit v4 on v3

--- a/solution.py
+++ b/solution.py
@@ -445,11 +445,9 @@
     )(source, pool, rest)
 
 
-def attend_kernel(
-    fast, where, wanted, info, query, pool, query_pool, out, part, stats,
-    fetched, asked, sems, asked_sems,
+def gather_kernel(
+    fast, where, wanted, info, pool, query_pool, fetched, asked, held, held_asked, sems, out_sems
 ):
-    head = pl.program_id(0)
     first = info[HEADS]
 
     def spot(code, h):
@@ -472,7 +470,7 @@
         far = (step * 2 + (rank & 1)) * SLOTS + (rank >> 1)
         return jnp.where(delta == 0, near, far)
 
-    def copies(h, slot):
+    def copies(h):
         for i in range(FETCH):
             if i < NEAR:
                 code = jnp.clip(first - WIN + i, 0, CODES - 1)
@@ -480,122 +478,86 @@
                 code = info[HEADS + 1 + i - NEAR]
             else:
                 code = wanted[h * PICKS + i - NEAR - G]
-            yield pltpu.make_async_copy(
-                pool.at[spot(code, h)], fetched.at[slot, i], sems.at[slot, i]
-            )
+            yield pltpu.make_async_copy(pool.at[spot(code, h)], held.at[h, i], sems.at[h, i])
         for g in range(G):
             yield pltpu.make_async_copy(
-                query_pool.at[query_spot(g, h), h % 2], asked.at[slot, g], asked_sems.at[slot, g]
+                query_pool.at[query_spot(g, h), h % 2], held_asked.at[h, g], sems.at[h, FETCH + g]
             )
 
-    @pl.when(head == 0)
-    def _():
-        for copy in copies(head, 0):
+    def start(h, carry):
+        for copy in copies(h):
             copy.start()
-
-    @pl.when(head + 1 < HEADS)
-    def _():
-        for copy in copies(head + 1, (head + 1) % 2):
+        return carry
+
+    def store(h):
+        return (
+            pltpu.make_async_copy(held.at[h], fetched.at[h], out_sems.at[h, 0]),
+            pltpu.make_async_copy(held_asked.at[h], asked.at[h], out_sems.at[h, 1]),
+        )
+
+    def pass_on(h, carry):
+        for i in range(FETCH):
+            pltpu.make_async_copy(pool.at[0], held.at[h, i], sems.at[h, i]).wait()
+        for g in range(G):
+            pltpu.make_async_copy(
+                query_pool.at[0, 0], held_asked.at[h, g], sems.at[h, FETCH + g]
+            ).wait()
+        for copy in store(h):
             copy.start()
-
-    slot = head % 2
-    for copy in copies(head, slot):
-        copy.wait()
-    radius = info[head]
-    column = lax.broadcasted_iota(jnp.int32, (1, WKEYS), 1) // BLOCK - WIN
-    contract = (((1,), (1,)), ((), ()))
-    scale = 1.0 / math.sqrt(WIDTH)
-
-    own = range(WIN, WIN + NB_DEV)
-    scores = scale * lax.dot_general(
-        jnp.concatenate([fetched[slot, i, 0] for i in own], axis=0),
-        asked[slot].reshape(G * BLOCK, WIDTH),
-        contract,
-        preferred_element_type=jnp.float32,
-    )
-    peak = jnp.max(scores, axis=0, keepdims=True)
-    weights = jnp.exp(scores - peak)
-    sums = jnp.sum(weights, axis=0, keepdims=True)
-    weighted = lax.dot_general(
-        jnp.concatenate([fetched[slot, i, 1] for i in own], axis=0),
-        weights.astype(jnp.bfloat16),
-        (((0,), (0,)), ((), ())),
-        preferred_element_type=jnp.float32,
-    )
-    part[0] = (weighted / sums).astype(jnp.bfloat16)
-    stats[0] = jnp.concatenate((peak, sums, jnp.zeros((6, WIDTH), jnp.float32)), axis=0)
-
-    def one_block(b, carry):
-        rows = pl.ds(pl.multiple_of(b * BLOCK, BLOCK), BLOCK)
-        q = query[0, rows]
-        window = [b + i for i in range(2 * WIN + 1)]
-        near_keys = jnp.concatenate([fetched[slot, i, 0] for i in window], axis=0)
-        near_values = jnp.concatenate([fetched[slot, i, 1] for i in window], axis=0)
-        others = [NEAR, NEAR + 1] + [NEAR + G + b * R + r for r in range(R)]
-        far_keys = jnp.concatenate([fetched[slot, i, 0] for i in others], axis=0)
-        far_values = jnp.concatenate([fetched[slot, i, 1] for i in others], axis=0)
-        target = first + b + column
-        usable = (jnp.abs(column) <= radius) & (target >= 0) & (target < CODES)
-        near = lax.dot_general(q, near_keys, contract, preferred_element_type=jnp.float32)
-        near = jnp.where(usable, near * scale, -jnp.inf)
-        far = lax.dot_general(q, far_keys, contract, preferred_element_type=jnp.float32) * scale
-        peak = jnp.maximum(
-            jnp.max(near, axis=1, keepdims=True), jnp.max(far, axis=1, keepdims=True)
-        )
-        near = jnp.exp(near - peak)
-        far = jnp.exp(far - peak)
-        row_total = jnp.sum(near, axis=1, keepdims=True) + jnp.sum(far, axis=1, keepdims=True)
-        weighted = jnp.dot(
-            near.astype(jnp.bfloat16), near_values, preferred_element_type=jnp.float32
-        ) + jnp.dot(far.astype(jnp.bfloat16), far_values, preferred_element_type=jnp.float32)
-        out[0, rows] = (weighted / row_total).astype(jnp.bfloat16)
         return carry
 
-    lax.fori_loop(0, NB_DEV, one_block, 0, unroll=2)
-
-
-def attend(fast, where, wanted, info, query, pool, query_pool):
-    per_head = lambda rows: pl.BlockSpec((1, rows, WIDTH), lambda h, *_: (h, 0, 0))
+    def finish(h, carry):
+        for copy in store(h):
+            copy.wait()
+        return carry
+
+    lax.fori_loop(0, HEADS, start, 0)
+    lax.fori_loop(0, HEADS, pass_on, 0)
+    lax.fori_loop(0, HEADS, finish, 0)
+
+
+def gather(fast, where, wanted, info, pool, query_pool):
+    smem = pl.BlockSpec(memory_space=pltpu.SMEM)
+    hbm = pl.BlockSpec(memory_space=pl.ANY)
     return pl.pallas_call(
-        lambda *refs: attend_kernel(fast, *refs),
-        grid_spec=pltpu.PrefetchScalarGridSpec(
-            num_scalar_prefetch=3,
-            grid=(HEADS,),
-            in_specs=[
-                per_head(NB_DEV * BLOCK),
-                pl.BlockSpec(memory_space=pl.ANY),
-                pl.BlockSpec(memory_space=pl.ANY),
-            ],
-            out_specs=(per_head(NB_DEV * BLOCK), per_head(WIDTH), per_head(8)),
-            scratch_shapes=[
-                pltpu.VMEM((2, FETCH) + UNIT, jnp.bfloat16),
-                pltpu.VMEM((2, G, BLOCK, WIDTH), jnp.bfloat16),
-                pltpu.SemaphoreType.DMA((2, FETCH)),
-                pltpu.SemaphoreType.DMA((2, G)),
-            ],
+        lambda *refs: gather_kernel(fast, *refs),
+        in_specs=[smem, smem, smem, hbm, hbm],
+        out_specs=(hbm, hbm),
+        out_shape=(
+            jax.ShapeDtypeStruct((HEADS, FETCH) + UNIT, jnp.bfloat16),
+            jax.ShapeDtypeStruct((HEADS, G, BLOCK, WIDTH), jnp.bfloat16),
         ),
-        out_shape=(
-            jax.ShapeDtypeStruct((HEADS, NB_DEV * BLOCK, WIDTH), jnp.bfloat16),
-            jax.ShapeDtypeStruct((HEADS, WIDTH, G * BLOCK), jnp.bfloat16),
-            jax.ShapeDtypeStruct((HEADS, 8, G * BLOCK), jnp.float32),
-        ),
+        scratch_shapes=[
+            pltpu.VMEM((HEADS, FETCH) + UNIT, jnp.bfloat16),
+            pltpu.VMEM((HEADS, G, BLOCK, WIDTH), jnp.bfloat16),
+            pltpu.SemaphoreType.DMA((HEADS, FETCH + G)),
+            pltpu.SemaphoreType.DMA((HEADS, 2)),
+        ],
         compiler_params=pltpu.CompilerParams(vmem_limit_bytes=32 * 1024 * 1024),
-        name="attend" if fast else "attend_gathered",
-    )(where, wanted, info, query, pool, query_pool)
+        name="gather" if fast else "gather_slow",
+    )(where, wanted, info, pool, query_pool)
 
 
 HALF = HEADS // 2
 SHARE = HALF * WIDTH // CHIPS
 
 
-def merge_kernel(
-    part, stats, merged, theirs, their_stats, half, half_stats, got, got_stats, piece,
-    pair_send, pair_land, send, land, send_stats, land_stats, back, home,
+def attend_kernel(
+    info, query, pairs, asked, fetched, out, merged,
+    held, part, stats, theirs, their_stats, half, half_stats, got, got_stats, piece,
+    load_sem, pair_send, pair_land, send, land, send_stats, land_stats, back, home,
 ):
     me = lax.axis_index("seq")
     chip, side = me // 2, lax.rem(me, 2)
     sibling = me + 1 - 2 * side
     peers = [lax.rem(chip + k, CHIPS) * 2 + side for k in range(1, CHIPS)]
+    first = me * NB_DEV
+
+    def load(h):
+        return pltpu.make_async_copy(fetched.at[h], held.at[h], load_sem.at[h])
+
+    for h in range(HEADS):
+        load(h).start()
     greet([place(peer) for peer in peers] + [place(sibling)])
 
     def pair(i, source, target):
@@ -608,6 +570,66 @@
             device_id_type=MESH,
         )
 
+    column = lax.broadcasted_iota(jnp.int32, (1, WKEYS), 1) // BLOCK - WIN
+    contract = (((1,), (1,)), ((), ()))
+    scale = 1.0 / math.sqrt(WIDTH)
+
+
+    def one_partial(h, carry):
+        own = pl.ds(h * NB_DEV, NB_DEV)
+        scores = scale * lax.dot_general(
+            pairs[own, 0].reshape(NB_DEV * BLOCK, WIDTH),
+            asked[h].reshape(G * BLOCK, WIDTH),
+            contract,
+            preferred_element_type=jnp.float32,
+        )
+        peak = jnp.max(scores, axis=0, keepdims=True)
+        weights = jnp.exp(scores - peak)
+        sums = jnp.sum(weights, axis=0, keepdims=True)
+        weighted = lax.dot_general(
+            pairs[own, 1].reshape(NB_DEV * BLOCK, WIDTH),
+            weights.astype(jnp.bfloat16),
+            (((0,), (0,)), ((), ())),
+            preferred_element_type=jnp.float32,
+        )
+        part[h] = (weighted / sums).astype(jnp.bfloat16)
+        stats[h] = jnp.concatenate((peak, sums, jnp.zeros((6, WIDTH), jnp.float32)), axis=0)
+        return carry
+
+    def one_head(head, outer):
+        load(head).wait()
+        radius = info[head]
+
+        def one_block(b, carry):
+            rows = pl.ds(pl.multiple_of(b * BLOCK, BLOCK), BLOCK)
+            q = query[head, rows]
+            window = [b + i for i in range(2 * WIN + 1)]
+            near_keys = jnp.concatenate([held[head, i, 0] for i in window], axis=0)
+            near_values = jnp.concatenate([held[head, i, 1] for i in window], axis=0)
+            others = [NEAR, NEAR + 1] + [NEAR + G + b * R + r for r in range(R)]
+            far_keys = jnp.concatenate([held[head, i, 0] for i in others], axis=0)
+            far_values = jnp.concatenate([held[head, i, 1] for i in others], axis=0)
+            target = first + b + column
+            usable = (jnp.abs(column) <= radius) & (target >= 0) & (target < CODES)
+            near = lax.dot_general(q, near_keys, contract, preferred_element_type=jnp.float32)
+            near = jnp.where(usable, near * scale, -jnp.inf)
+            far = lax.dot_general(q, far_keys, contract, preferred_element_type=jnp.float32) * scale
+            peak = jnp.maximum(
+                jnp.max(near, axis=1, keepdims=True), jnp.max(far, axis=1, keepdims=True)
+            )
+            near = jnp.exp(near - peak)
+            far = jnp.exp(far - peak)
+            row_total = jnp.sum(near, axis=1, keepdims=True) + jnp.sum(far, axis=1, keepdims=True)
+            weighted = jnp.dot(
+                near.astype(jnp.bfloat16), near_values, preferred_element_type=jnp.float32
+            ) + jnp.dot(far.astype(jnp.bfloat16), far_values, preferred_element_type=jnp.float32)
+            out[head, rows] = (weighted / row_total).astype(jnp.bfloat16)
+            return carry
+
+        lax.fori_loop(0, NB_DEV, one_block, 0, unroll=2)
+        return outer
+
+    lax.fori_loop(0, HEADS, one_partial, 0)
     their_heads = pl.ds((1 - side) * HALF, HALF)
     my_heads = pl.ds(side * HALF, HALF)
     swaps = [
@@ -616,6 +638,7 @@
     ]
     for copy in swaps:
         copy.start()
+    lax.fori_loop(0, 1, one_head, 0)
     for copy in swaps:
         copy.wait_recv()
     for h in range(HALF):
@@ -673,6 +696,7 @@
     head, span = rows(chip)
     got[chip] = half[head, span]
     got_stats[chip] = half_stats[...]
+    lax.fori_loop(1, 4, one_head, 0)
     for k in range(1, CHIPS):
         for copy in hand(k, lax.rem(chip + CHIPS - k, CHIPS)):
             copy.wait_recv()
@@ -691,10 +715,12 @@
     for k in range(1, CHIPS):
         give(k, chip).start()
     merged[side * HALF + head, span] = piece[...]
+    lax.fori_loop(4, 7, one_head, 0)
     for k in range(1, CHIPS):
         give(k, lax.rem(chip + CHIPS - k, CHIPS)).wait_recv()
     last = pair(2, merged.at[my_heads], merged.at[my_heads])
     last.start()
+    lax.fori_loop(7, HEADS, one_head, 0)
     for copy in swaps:
         copy.wait_send()
     for k in range(1, CHIPS):
@@ -705,16 +731,25 @@
     pair(2, merged.at[their_heads], merged.at[their_heads]).wait_recv()
 
 
-def merge(part, stats):
+def attend(info, query, pairs, asked, fetched):
     dma = pltpu.SemaphoreType.DMA
     vmem = pl.BlockSpec(memory_space=pltpu.VMEM)
     rows = G * BLOCK
     return pl.pallas_call(
-        merge_kernel,
-        in_specs=[vmem, vmem],
-        out_specs=vmem,
-        out_shape=jax.ShapeDtypeStruct((HEADS, WIDTH, rows), jnp.bfloat16),
+        attend_kernel,
+        in_specs=[
+            pl.BlockSpec(memory_space=pltpu.SMEM), vmem, vmem, vmem,
+            pl.BlockSpec(memory_space=pl.ANY),
+        ],
+        out_specs=(vmem, vmem),
+        out_shape=(
+            jax.ShapeDtypeStruct((HEADS, NB_DEV * BLOCK, WIDTH), jnp.bfloat16),
+            jax.ShapeDtypeStruct((HEADS, WIDTH, rows), jnp.bfloat16),
+        ),
         scratch_shapes=[
+            pltpu.VMEM((HEADS, FETCH) + UNIT, jnp.bfloat16),
+            pltpu.VMEM((HEADS, WIDTH, rows), jnp.bfloat16),
+            pltpu.VMEM((HEADS, 8, rows), jnp.float32),
             pltpu.VMEM((HALF, WIDTH, rows), jnp.bfloat16),
             pltpu.VMEM((HALF, 8, rows), jnp.float32),
             pltpu.VMEM((HALF, WIDTH, rows), jnp.bfloat16),
@@ -722,12 +757,15 @@
             pltpu.VMEM((CHIPS, SHARE, rows), jnp.bfloat16),
             pltpu.VMEM((CHIPS, 2 * HALF, rows), jnp.float32),
             pltpu.VMEM((SHARE, rows), jnp.bfloat16),
+            dma((HEADS,)),
         ]
         + [dma((3,))] * 2
         + [dma((CHIPS,))] * 6,
-        compiler_params=pltpu.CompilerParams(collective_id=2, has_side_effects=True),
-        name="merge",
-    )(part, stats)
+        compiler_params=pltpu.CompilerParams(
+            collective_id=2, has_side_effects=True, vmem_limit_bytes=32 * 1024 * 1024
+        ),
+        name="attend",
+    )(info, query, pairs, asked, fetched)
 
 
 def local(queries, keys, values, window_radius, global_ids, rand_owner, rand_local):
@@ -751,21 +789,20 @@
     source, where, rest = plan(global_ids, table, radius)
     log, flag = packets(source, pool, rest)
     info = jnp.concatenate((window_radius, (position * NB_DEV)[None], global_ids)).astype(jnp.int32)
-    rest_args = (where, wanted.reshape(-1), info, query_heads)
+    asking = (where, wanted.reshape(-1), info)
 
     def from_packets(pairs, units, log):
-        return attend(True, *rest_args, log, log)
+        return gather(True, *asking, log, log)
 
     def from_gather(pairs, units, log):
         everything = lax.all_gather(pairs, "seq", axis=0, tiled=True)
         holder = jnp.repeat(global_ids // NB_DEV, QUNITS // G) == position
         asked = lax.psum(jnp.where(holder[:, None, None, None], units, 0), "seq")
-        return attend(False, *rest_args, everything, asked)
-
-    sparse, part, stats = lax.cond(
-        jnp.max(flag) > 0, from_gather, from_packets, pairs, units, log
-    )
-    global_out = merge(part, stats).reshape(HEADS, WIDTH, G, BLOCK).transpose(2, 3, 0, 1)
+        return gather(False, *asking, everything, asked)
+
+    fetched, asked = lax.cond(jnp.max(flag) > 0, from_gather, from_packets, pairs, units, log)
+    sparse, merged = attend(info, query_heads, pairs, asked, fetched)
+    global_out = merged.reshape(HEADS, WIDTH, G, BLOCK).transpose(2, 3, 0, 1)
 
     result = sparse.reshape(HEADS, NB_DEV, BLOCK, WIDTH).transpose(1, 2, 0, 3)
     for slot in range(G):

time: 368 us -> 353 us (0.959)
  Pallas kernels: 332 us -> 317 us
    pallas_call x2, Pallas kernels: 67.1 us -> 52.1 us  [the longest x1 40.5 us: attend(): pl.pallas_call(attend_kernel, in_specs=[pl.BlockSpec(memory_space=pltpu.S...]
where the time goes in v4:
time: 353 us; the launch traced here: 352 us
  Pallas kernels  317 us (90%)
  between operations  18 us (5%)
  local copies, waits for them, and re-layouts  13.5 us (4%)
  other arithmetic  3.8 us (1%)
    pallas_call x1, Pallas kernels, packets(): pl.pallas_call(packet_kernel, in_specs=[pl.BlockSpec(memory_space=pltpu.S...  224 us
    pallas_call x1, Pallas kernels, attend(): pl.pallas_call(attend_kernel, in_specs=[pl.BlockSpec(memory_space=pltpu.S...  40.5 us
    pallas_call x1, Pallas kernels, exchange(): pl.pallas_call(exchange_kernel, in_specs=[vmem, hbm, hbm], out_specs=(vme...  25.4 us
    pallas_call x1, Pallas kernels, plan(): pl.pallas_call(plan_kernel, in_specs=[smem, vmem, vmem], out_specs=(smem,...  15.6 us
    pallas_call x1, Pallas kernels, gather(): pl.pallas_call(lambda *refs: gather_kernel(fast, *refs), in_specs=[smem,...  11.6 us

profile of v4, /device:TPU:1, one launch (start us, length us, event | category | flops | bytes accessed | tf_op | source)
XLA Modules:
  0.0 352.5 jit_solution(1175846656553995840)
XLA Ops:
  6.5 0.8 pad_add_fusion.info
  7.3 1.3 fusion.4
  12.4 1.3 fusion.1
  13.7 1.3 broadcast_in_dim.59.radius
  15.0 0.7 add_bitcast_fusion
  15.8 0.1 copy.31
  15.9 0.6 pad.4.wanted
  16.4 0.1 copy.32
  16.6 0.1 reshape_reshape.3
  16.7 1.4 copy.43
  18.2 1.5 copy.28
  19.6 1.5 copy.29
  21.1 0.2 pad_maximum_fusion
  21.3 0.0 copy-start.4
  21.4 25.4 %exchange.1 = (s32[32,8,128]{2,1,0:T(8,128)}, bf16[144,2,64,128]{3,2,1,0:T(8,128)(2,1)}) custom-call(s32[8,128]{1,0:T(8,128)} %pad.4.wanted, bf16[64,2,64,128]{3,2,1,0:T(8,128)(2,1)S(1)} %bitcast.37, bf16[8,2,64,128]{3,2,1,0:T(8,128)(2,1)S(1)} %bitcast.40), custom_call_target="tpu_custom_call" | custom-call | tf_op jit(solution)/shard_map/exchange/pallas_call | solution.py:100
  46.8 0.0 copy-done.6
  46.8 15.6 %plan.1 = (s32[592]{0:T(1024)}, s32[8,256]{1,0:T(8,128)S(1)}, s32[8,128]{1,0:T(8,128)}) custom-call(s32[2]{0:T(128)S(1)} %copy-done.6, s32[32,8,128]{2,1,0:T(8,128)} %get-tuple-element.49.table, s32[8,256]{1,0:T(8,128)} %broadcast_in_dim.59.radius), custom_call_target="tpu_custom_call" | custom-call | tf_op jit(solution)/shard_map/plan/pallas_call | solution.py:265
  62.4 0.0 copy-start
  62.4 2.3 copy-done
  64.7 0.0 copy-start.2
  64.7 0.7 copy-done.2
  65.4 0.0 copy-start.3
  65.4 0.7 copy-done.3
  66.1 224.0 %packets.1 = (bf16[1328,2,64,128]{3,2,1,0:T(8,128)(2,1)}, s32[8,128]{1,0:T(8,128)S(1)}) custom-call(s32[592]{0:T(1024)S(1)} %copy-done.2, bf16[144,2,64,128]{3,2,1,0:T(8,128)(2,1)S(1)} %copy-done, s32[8,128]{1,0:T(8,128)S(1)} %copy-done.3), custom_call_target="tpu_custom_call" | custom-call | tf_op jit(solution)/shard_map/packets/pallas_call | solution.py:416
  290.1 0.6 reduce_max.9
  291.4 0.0 copy-done.4
  291.4 11.6 %conditional.1 = ((bf16[8,40,2,64,128]{4,3,2,1,0:T(8,128)(2,1)}, bf16[8,2,64,128]{3,2,1,0:T(8,128)(2,1)S(1)})) conditional(s32[]{:T(128)} %convert_element_type.5, (s32[8,256]{1,0:T(8,128)S(1)}, s32[192]{0:T(256)S(1)}, s32[11]{0:T(128)S(1)}, bf16[1328,2,64,128]{3,2,1,0:T(8,128)(2,1)}) %tuple.11, (bf16[64,2,64,128]{3,2,1,0:T(8,128)(2,1)S(1)}, ...), branch_computations={%region_1.2_spmd, %region_2.4_spmd} | conditional | flops 262176 | bytes 219152576 | solution.py:803
  291.4 11.6 %gather.1 = (bf16[8,40,2,64,128]{4,3,2,1,0:T(8,128)(2,1)}, bf16[8,2,64,128]{3,2,1,0:T(8,128)(2,1)S(1)}) custom-call(s32[8,256]{1,0:T(8,128)S(1)} %get-tuple-element.27.refs_0_, s32[192]{0:T(256)S(1)} %get-tuple-element.28.refs_1_, s32[11]{0:T(128)S(1)} %get-tuple-element.29.refs_2_, bf16[1328,2,64,128]{3,2,1,0:T(8,128)(2,1)} %get-tuple-element.30.refs_3_.refs_4_, ...), custom_call_target="tpu_custom_call" | custom-call | tf_op jit(solution)/shard_map/cond/branch_0_fun/gather/pallas_call | solution.py:522
  303.0 40.5 %attend.1 = (bf16[8,512,128]{2,1,0:T(8,128)(2,1)S(1)}, bf16[8,128,128]{2,1,0:T(8,128)(2,1)S(1)}) custom-call(s32[11]{0:T(128)S(1)} %pad_add_fusion.info, bf16[8,512,128]{2,1,0:T(8,128)(2,1)S(1)} %bitcast.35, bf16[64,2,64,128]{3,2,1,0:T(8,128)(2,1)} %bitcast.39, bf16[8,2,64,128]{3,2,1,0:T(8,128)(2,1)S(1)} %get-tuple-element.56.asked, ...), custom_call_target="tpu_custom_call" | custom-call | tf_op jit(solution)/shard_map/attend/pallas_call | solution.py:738
  343.6 0.2 copy.33
  343.8 0.2 select_select_fusion
  343.9 1.7 copy.38
  (6 shorter events, 0.1 us)
Async XLA Ops:
  6.5 40.2 %copy-start.6 = (s32[2]{0:T(128)S(1)}, s32[2]{0:T(128)}, u32[]{:S(2)}) copy-start(s32[2]{0:T(128)} %global_ids.1) | copy-start | bytes 28
  21.3 270.1 %copy-start.4 = (bf16[2,8,64,8,128]{4,2,0,1,3:T(8,128)(2,1)}, bf16[2,8,64,8,128]{4,2,0,1,3:T(8,128)(2,1)S(1)}, u32[]{:S(2)}) copy-start(bf16[2,8,64,8,128]{4,2,0,1,3:T(8,128)(2,1)S(1)} %pad_maximum_fusion) | copy-start | bytes 6291460
  62.4 2.3 copy-start
  64.7 0.7 copy-start.2
  65.4 0.7 copy-start.3

commit v5 on v4

--- a/solution.py
+++ b/solution.py
@@ -14,7 +14,7 @@
 NB_DEV = 8
 HEADS = 8
 WIDTH = 128
-WKEYS = (2 * WIN + 1) * BLOCK
+LISTED = 2 * WIN + 1 + G + R
 PICKS = NB_DEV * R
 NEAR = NB_DEV + 2 * WIN
 FETCH = NEAR + G + PICKS
@@ -26,7 +26,7 @@
 QUNITS = 8
 UNITS = 2 * QUNITS + 2 * OWN
 SLOTS = 8
-PHASES = 37
+PHASES = 36
 PIECES = 4
 PIECE = SLOTS // PIECES
 STAGES = 4
@@ -183,7 +183,7 @@
         after = []
         for way in range(2):
             rank, reach = ways[way][0], reaches_wide[way]
-            going, queue, start, slot = state[4 * way : 4 * way + 4]
+            going, queue, key = state[3 * way : 3 * way + 3]
             free = (going == 0).astype(jnp.int32)
             running = running_rows(free)
             nth = running - free
@@ -195,24 +195,23 @@
             mark = jnp.where(fresh, number, -1)
             for s in range(2 * SLOTS):
                 here = rank == jnp.broadcast_to(mark[s : s + 1, :], shape)
-                start = jnp.where(here, t, start)
-                slot = jnp.where(here, s, slot)
+                key = jnp.where(here, t * 2 * SLOTS + s, key)
             going = jnp.maximum(pltpu.roll(going, 16 if way == 0 else CODES - 16, 1) - 1, 0)
-            after += [going, taken, start, slot]
+            after += [going, taken, key]
         return tuple(after)
 
-    state = lax.fori_loop(0, PHASES, phase, (wide(zero), wide(zero), zero, zero) * 2)
+    state = lax.fori_loop(0, PHASES, phase, (wide(zero), wide(zero), zero) * 2)
     over = wide(zero)
     for way in range(2):
-        over = over + state[4 * way] + reaches_wide[way][1] - state[4 * way + 1]
+        over = over + state[3 * way] + reaches_wide[way][1] - state[3 * way + 1]
     over = over[:HEADS] + over[HEADS:]
     rest[...] = over[:, :128] + over[:, 128:]
 
     delta = (chip - home) & (CHIPS - 1)
     core = (code >> 3) & 1
     near = ENTRIES + 2 * QUNITS + core * OWN + row * NB_DEV + (code & 7)
-    goes = [state[2] + delta - 1, PHASES + state[6] + CHIPS - delta - 1]
-    slots = [state[3], state[7]]
+    goes = [(state[2] >> 4) + delta - 1, PHASES + (state[5] >> 4) + CHIPS - delta - 1]
+    slots = [state[2] & 15, state[5] & 15]
     entry = [(goes[way] * 2 + (slots[way] & 1)) * SLOTS + (slots[way] >> 1) for way in range(2)]
     from_left = (delta < 8) | ((delta == 8) & (right == 8))
     far_entry = jnp.clip(jnp.where(from_left, entry[0], entry[1]), 0, ENTRIES - 1)
@@ -220,8 +219,8 @@
 
     for way in range(2):
         rank, reach = ways[way]
-        sent = rank < state[4 * way + 1][:HEADS]
-        keys[way] = jnp.where(sent, state[4 * way + 2] * 2 * SLOTS + state[4 * way + 3], -1)
+        sent = rank < state[3 * way + 1][:HEADS]
+        keys[way] = jnp.where(sent, state[3 * way + 2], -1)
     fetch = pltpu.make_async_copy(keys, numbers, sems)
     fetch.start()
     fetch.wait()
@@ -570,7 +569,7 @@
             device_id_type=MESH,
         )
 
-    column = lax.broadcasted_iota(jnp.int32, (1, WKEYS), 1) // BLOCK - WIN
+    column = lax.broadcasted_iota(jnp.int32, (1, LISTED * BLOCK), 1) // BLOCK - WIN
     contract = (((1,), (1,)), ((), ()))
     scale = 1.0 / math.sqrt(WIDTH)
 
@@ -602,31 +601,26 @@
 
         def one_block(b, carry):
             rows = pl.ds(pl.multiple_of(b * BLOCK, BLOCK), BLOCK)
-            q = query[head, rows]
-            window = [b + i for i in range(2 * WIN + 1)]
-            near_keys = jnp.concatenate([held[head, i, 0] for i in window], axis=0)
-            near_values = jnp.concatenate([held[head, i, 1] for i in window], axis=0)
-            others = [NEAR, NEAR + 1] + [NEAR + G + b * R + r for r in range(R)]
-            far_keys = jnp.concatenate([held[head, i, 0] for i in others], axis=0)
-            far_values = jnp.concatenate([held[head, i, 1] for i in others], axis=0)
+            units = [b + i for i in range(2 * WIN + 1)] + [NEAR, NEAR + 1]
+            units = units + [NEAR + G + b * R + r for r in range(R)]
+            held_keys = jnp.concatenate([held[head, i, 0] for i in units], axis=0)
+            held_values = jnp.concatenate([held[head, i, 1] for i in units], axis=0)
             target = first + b + column
-            usable = (jnp.abs(column) <= radius) & (target >= 0) & (target < CODES)
-            near = lax.dot_general(q, near_keys, contract, preferred_element_type=jnp.float32)
-            near = jnp.where(usable, near * scale, -jnp.inf)
-            far = lax.dot_general(q, far_keys, contract, preferred_element_type=jnp.float32) * scale
-            peak = jnp.maximum(
-                jnp.max(near, axis=1, keepdims=True), jnp.max(far, axis=1, keepdims=True)
+            inside = (jnp.abs(column) <= radius) & (target >= 0) & (target < CODES)
+            usable = inside | (column > WIN)
+            scores = scale * lax.dot_general(
+                query[head, rows], held_keys, contract, preferred_element_type=jnp.float32
             )
-            near = jnp.exp(near - peak)
-            far = jnp.exp(far - peak)
-            row_total = jnp.sum(near, axis=1, keepdims=True) + jnp.sum(far, axis=1, keepdims=True)
+            scores = jnp.where(usable, scores, -jnp.inf)
+            weights = jnp.exp(scores - jnp.max(scores, axis=1, keepdims=True))
+            row_total = jnp.sum(weights, axis=1, keepdims=True)
             weighted = jnp.dot(
-                near.astype(jnp.bfloat16), near_values, preferred_element_type=jnp.float32
-            ) + jnp.dot(far.astype(jnp.bfloat16), far_values, preferred_element_type=jnp.float32)
+                weights.astype(jnp.bfloat16), held_values, preferred_element_type=jnp.float32
+            )
             out[head, rows] = (weighted / row_total).astype(jnp.bfloat16)
             return carry
 
-        lax.fori_loop(0, NB_DEV, one_block, 0, unroll=2)
+        lax.fori_loop(0, NB_DEV, one_block, 0, unroll=4)
         return outer
 
     lax.fori_loop(0, HEADS, one_partial, 0)

time: 353 us -> 346 us (0.980)
  Pallas kernels: 317 us -> 310 us
    pallas_call x1, Pallas kernels: 224 us -> 218 us  [packets(): pl.pallas_call(packet_kernel, in_specs=[pl.BlockSpec(memory_space=pltpu.S...]
where the time goes in v5:
time: 346 us; the launch traced here: 345 us
  Pallas kernels  310 us (90%)
  between operations  18 us (5%)
  local copies, waits for them, and re-layouts  13.5 us (4%)
  other arithmetic  3.8 us (1%)
    pallas_call x1, Pallas kernels, packets(): pl.pallas_call(packet_kernel, in_specs=[pl.BlockSpec(memory_space=pltpu.S...  218 us
    pallas_call x1, Pallas kernels, attend(): pl.pallas_call(attend_kernel, in_specs=[pl.BlockSpec(memory_space=pltpu.S...  39.3 us
    pallas_call x1, Pallas kernels, exchange(): pl.pallas_call(exchange_kernel, in_specs=[vmem, hbm, hbm], out_specs=(vme...  25.4 us
    pallas_call x1, Pallas kernels, plan(): pl.pallas_call(plan_kernel, in_specs=[smem, vmem, vmem], out_specs=(smem,...  15.1 us
    pallas_call x1, Pallas kernels, gather(): pl.pallas_call(lambda *refs: gather_kernel(fast, *refs), in_specs=[smem,...  11.7 us

profile of v5, /device:TPU:1, one launch (start us, length us, event | category | flops | bytes accessed | tf_op | source)
XLA Modules:
  0.0 345.2 jit_solution(11307609118148134025)
XLA Ops:
  6.5 0.8 pad_add_fusion.info
  7.3 1.3 fusion.4
  12.4 1.3 fusion.1
  13.7 1.3 broadcast_in_dim.59.radius
  15.0 0.7 add_bitcast_fusion
  15.8 0.1 copy.31
  15.9 0.6 pad.4.wanted
  16.4 0.1 copy.32
  16.6 0.1 reshape_reshape.3
  16.7 1.4 copy.43
  18.2 1.5 copy.28
  19.6 1.5 copy.29
  21.1 0.2 pad_maximum_fusion
  21.3 0.0 copy-start.4
  21.4 25.4 %exchange.1 = (s32[32,8,128]{2,1,0:T(8,128)}, bf16[144,2,64,128]{3,2,1,0:T(8,128)(2,1)}) custom-call(s32[8,128]{1,0:T(8,128)} %pad.4.wanted, bf16[64,2,64,128]{3,2,1,0:T(8,128)(2,1)S(1)} %bitcast.37, bf16[8,2,64,128]{3,2,1,0:T(8,128)(2,1)S(1)} %bitcast.40), custom_call_target="tpu_custom_call" | custom-call | tf_op jit(solution)/shard_map/exchange/pallas_call | solution.py:100
  46.8 0.0 copy-done.6
  46.8 15.1 %plan.1 = (s32[576]{0:T(1024)}, s32[8,256]{1,0:T(8,128)S(1)}, s32[8,128]{1,0:T(8,128)}) custom-call(s32[2]{0:T(128)S(1)} %copy-done.6, s32[32,8,128]{2,1,0:T(8,128)} %get-tuple-element.49.table, s32[8,256]{1,0:T(8,128)} %broadcast_in_dim.59.radius), custom_call_target="tpu_custom_call" | custom-call | tf_op jit(solution)/shard_map/plan/pallas_call | solution.py:264
  61.9 0.0 copy-start
  61.9 2.3 copy-done
  64.3 0.0 copy-start.2
  64.3 0.7 copy-done.2
  64.9 0.0 copy-start.3
  64.9 0.7 copy-done.3
  65.6 218.3 %packets.1 = (bf16[1296,2,64,128]{3,2,1,0:T(8,128)(2,1)}, s32[8,128]{1,0:T(8,128)S(1)}) custom-call(s32[576]{0:T(1024)S(1)} %copy-done.2, bf16[144,2,64,128]{3,2,1,0:T(8,128)(2,1)S(1)} %copy-done, s32[8,128]{1,0:T(8,128)S(1)} %copy-done.3), custom_call_target="tpu_custom_call" | custom-call | tf_op jit(solution)/shard_map/packets/pallas_call | solution.py:415
  284.0 0.6 reduce_max.9
  285.2 0.0 copy-done.4
  285.2 11.7 %conditional.1 = ((bf16[8,40,2,64,128]{4,3,2,1,0:T(8,128)(2,1)}, bf16[8,2,64,128]{3,2,1,0:T(8,128)(2,1)S(1)})) conditional(s32[]{:T(128)} %convert_element_type.5, (s32[8,256]{1,0:T(8,128)S(1)}, s32[192]{0:T(256)S(1)}, s32[11]{0:T(128)S(1)}, bf16[1296,2,64,128]{3,2,1,0:T(8,128)(2,1)}) %tuple.11, (bf16[64,2,64,128]{3,2,1,0:T(8,128)(2,1)S(1)}, ...), branch_computations={%region_1.2_spmd, %region_2.4_spmd} | conditional | flops 262176 | bytes 219152576 | solution.py:797
  285.3 11.7 %gather.1 = (bf16[8,40,2,64,128]{4,3,2,1,0:T(8,128)(2,1)}, bf16[8,2,64,128]{3,2,1,0:T(8,128)(2,1)S(1)}) custom-call(s32[8,256]{1,0:T(8,128)S(1)} %get-tuple-element.27.refs_0_, s32[192]{0:T(256)S(1)} %get-tuple-element.28.refs_1_, s32[11]{0:T(128)S(1)} %get-tuple-element.29.refs_2_, bf16[1296,2,64,128]{3,2,1,0:T(8,128)(2,1)} %get-tuple-element.30.refs_3_.refs_4_, ...), custom_call_target="tpu_custom_call" | custom-call | tf_op jit(solution)/shard_map/cond/branch_0_fun/gather/pallas_call | solution.py:521
  296.9 39.3 %attend.1 = (bf16[8,512,128]{2,1,0:T(8,128)(2,1)S(1)}, bf16[8,128,128]{2,1,0:T(8,128)(2,1)S(1)}) custom-call(s32[11]{0:T(128)S(1)} %pad_add_fusion.info, bf16[8,512,128]{2,1,0:T(8,128)(2,1)S(1)} %bitcast.35, bf16[64,2,64,128]{3,2,1,0:T(8,128)(2,1)} %bitcast.39, bf16[8,2,64,128]{3,2,1,0:T(8,128)(2,1)S(1)} %get-tuple-element.56.asked, ...), custom_call_target="tpu_custom_call" | custom-call | tf_op jit(solution)/shard_map/attend/pallas_call | solution.py:732
  336.3 0.2 copy.33
  336.5 0.2 select_select_fusion
  336.6 1.7 copy.38
  (6 shorter events, 0.1 us)
Async XLA Ops:
  6.5 40.2 %copy-start.6 = (s32[2]{0:T(128)S(1)}, s32[2]{0:T(128)}, u32[]{:S(2)}) copy-start(s32[2]{0:T(128)} %global_ids.1) | copy-start | bytes 28
  21.3 263.9 %copy-start.4 = (bf16[2,8,64,8,128]{4,2,0,1,3:T(8,128)(2,1)}, bf16[2,8,64,8,128]{4,2,0,1,3:T(8,128)(2,1)S(1)}, u32[]{:S(2)}) copy-start(bf16[2,8,64,8,128]{4,2,0,1,3:T(8,128)(2,1)S(1)} %pad_maximum_fusion) | copy-start | bytes 6291460
  61.9 2.3 copy-start
  64.3 0.7 copy-start.2
  64.9 0.7 copy-start.3

commit v6 on v5

--- a/solution.py
+++ b/solution.py
@@ -623,7 +623,7 @@
         lax.fori_loop(0, NB_DEV, one_block, 0, unroll=4)
         return outer
 
-    lax.fori_loop(0, HEADS, one_partial, 0)
+    lax.fori_loop(0, HEADS, one_partial, 0, unroll=4)
     their_heads = pl.ds((1 - side) * HALF, HALF)
     my_heads = pl.ds(side * HALF, HALF)
     swaps = [

time: 346 us -> 344 us (level)
  no operation moved by 1% of the time
where the time goes in v6:
time: 344 us; the launch traced here: 343 us
  Pallas kernels  308 us (90%)
  between operations  18 us (5%)
  local copies, waits for them, and re-layouts  13.5 us (4%)
  other arithmetic  3.8 us (1%)
    pallas_call x1, Pallas kernels, packets(): pl.pallas_call(packet_kernel, in_specs=[pl.BlockSpec(memory_space=pltpu.S...  218 us
    pallas_call x1, Pallas kernels, attend(): pl.pallas_call(attend_kernel, in_specs=[pl.BlockSpec(memory_space=pltpu.S...  37.3 us
    pallas_call x1, Pallas kernels, exchange(): pl.pallas_call(exchange_kernel, in_specs=[vmem, hbm, hbm], out_specs=(vme...  25.4 us
    pallas_call x1, Pallas kernels, plan(): pl.pallas_call(plan_kernel, in_specs=[smem, vmem, vmem], out_specs=(smem,...  15.1 us
    pallas_call x1, Pallas kernels, gather(): pl.pallas_call(lambda *refs: gather_kernel(fast, *refs), in_specs=[smem,...  11.7 us

profile of v6, /device:TPU:1, one launch (start us, length us, event | category | flops | bytes accessed | tf_op | source)
XLA Modules:
  0.0 343.4 jit_solution(821728257735676920)
XLA Ops:
  6.5 0.0 copy-start.6
  6.5 0.8 pad_add_fusion.info
  7.3 1.3 fusion.4
  12.4 1.3 fusion.1
  13.7 1.3 broadcast_in_dim.59.radius
  15.0 0.7 add_bitcast_fusion
  15.8 0.1 copy.31
  15.9 0.6 pad.4.wanted
  16.4 0.1 copy.32
  16.6 0.1 reshape_reshape.3
  16.7 1.4 copy.43
  18.2 1.5 copy.28
  19.6 1.5 copy.29
  21.1 0.2 pad_maximum_fusion
  21.3 0.0 copy-start.4
  21.4 25.4 %exchange.1 = (s32[32,8,128]{2,1,0:T(8,128)}, bf16[144,2,64,128]{3,2,1,0:T(8,128)(2,1)}) custom-call(s32[8,128]{1,0:T(8,128)} %pad.4.wanted, bf16[64,2,64,128]{3,2,1,0:T(8,128)(2,1)S(1)} %bitcast.37, bf16[8,2,64,128]{3,2,1,0:T(8,128)(2,1)S(1)} %bitcast.40), custom_call_target="tpu_custom_call" | custom-call | tf_op jit(solution)/shard_map/exchange/pallas_call | solution.py:100
  46.8 0.0 copy-done.6
  46.8 15.1 %plan.1 = (s32[576]{0:T(1024)}, s32[8,256]{1,0:T(8,128)S(1)}, s32[8,128]{1,0:T(8,128)}) custom-call(s32[2]{0:T(128)S(1)} %copy-done.6, s32[32,8,128]{2,1,0:T(8,128)} %get-tuple-element.49.table, s32[8,256]{1,0:T(8,128)} %broadcast_in_dim.59.radius), custom_call_target="tpu_custom_call" | custom-call | tf_op jit(solution)/shard_map/plan/pallas_call | solution.py:264
  61.9 0.0 copy-start
  61.9 2.3 copy-done
  64.3 0.0 copy-start.2
  64.3 0.7 copy-done.2
  64.9 0.7 copy-done.3
  65.6 218.3 %packets.1 = (bf16[1296,2,64,128]{3,2,1,0:T(8,128)(2,1)}, s32[8,128]{1,0:T(8,128)S(1)}) custom-call(s32[576]{0:T(1024)S(1)} %copy-done.2, bf16[144,2,64,128]{3,2,1,0:T(8,128)(2,1)S(1)} %copy-done, s32[8,128]{1,0:T(8,128)S(1)} %copy-done.3), custom_call_target="tpu_custom_call" | custom-call | tf_op jit(solution)/shard_map/packets/pallas_call | solution.py:415
  284.0 0.6 reduce_max.9
  285.2 0.0 copy-done.4
  285.2 11.9 %conditional.1 = ((bf16[8,40,2,64,128]{4,3,2,1,0:T(8,128)(2,1)}, bf16[8,2,64,128]{3,2,1,0:T(8,128)(2,1)S(1)})) conditional(s32[]{:T(128)} %convert_element_type.5, (s32[8,256]{1,0:T(8,128)S(1)}, s32[192]{0:T(256)S(1)}, s32[11]{0:T(128)S(1)}, bf16[1296,2,64,128]{3,2,1,0:T(8,128)(2,1)}) %tuple.11, (bf16[64,2,64,128]{3,2,1,0:T(8,128)(2,1)S(1)}, ...), branch_computations={%region_1.2_spmd, %region_2.4_spmd} | conditional | flops 262176 | bytes 219152576 | solution.py:797
  285.3 11.7 %gather.1 = (bf16[8,40,2,64,128]{4,3,2,1,0:T(8,128)(2,1)}, bf16[8,2,64,128]{3,2,1,0:T(8,128)(2,1)S(1)}) custom-call(s32[8,256]{1,0:T(8,128)S(1)} %get-tuple-element.27.refs_0_, s32[192]{0:T(256)S(1)} %get-tuple-element.28.refs_1_, s32[11]{0:T(128)S(1)} %get-tuple-element.29.refs_2_, bf16[1296,2,64,128]{3,2,1,0:T(8,128)(2,1)} %get-tuple-element.30.refs_3_.refs_4_, ...), custom_call_target="tpu_custom_call" | custom-call | tf_op jit(solution)/shard_map/cond/branch_0_fun/gather/pallas_call | solution.py:521
  297.2 37.3 %attend.1 = (bf16[8,512,128]{2,1,0:T(8,128)(2,1)S(1)}, bf16[8,128,128]{2,1,0:T(8,128)(2,1)S(1)}) custom-call(s32[11]{0:T(128)S(1)} %pad_add_fusion.info, bf16[8,512,128]{2,1,0:T(8,128)(2,1)S(1)} %bitcast.35, bf16[64,2,64,128]{3,2,1,0:T(8,128)(2,1)} %bitcast.39, bf16[8,2,64,128]{3,2,1,0:T(8,128)(2,1)S(1)} %get-tuple-element.56.asked, ...), custom_call_target="tpu_custom_call" | custom-call | tf_op jit(solution)/shard_map/attend/pallas_call | solution.py:732
  334.5 0.2 copy.33
  334.7 0.2 select_select_fusion
  334.9 1.7 copy.38
  (6 shorter events, 0.1 us)
Async XLA Ops:
  6.5 40.2 %copy-start.6 = (s32[2]{0:T(128)S(1)}, s32[2]{0:T(128)}, u32[]{:S(2)}) copy-start(s32[2]{0:T(128)} %global_ids.1) | copy-start | bytes 28
  21.3 263.9 %copy-start.4 = (bf16[2,8,64,8,128]{4,2,0,1,3:T(8,128)(2,1)}, bf16[2,8,64,8,128]{4,2,0,1,3:T(8,128)(2,1)S(1)}, u32[]{:S(2)}) copy-start(bf16[2,8,64,8,128]{4,2,0,1,3:T(8,128)(2,1)S(1)} %pad_maximum_fusion) | copy-start | bytes 6291460
  61.9 2.3 copy-start
  64.3 0.7 copy-start.2
  64.9 0.7 copy-start.3
